TPU v7x, 256 devices: a whole 4x4x8 slice. The times are simulated.
256 devices in a mesh: dom: 64 (over z, x, core), feat: 4 (over y).
Axes of the slice: x: 4, y: 4, z: 8, core: 2. Of those that a mesh axis runs over, the one named last changes fastest.
Arguments:
- feats: bfloat16 [16384, 1024], P('dom', 'feat'), may hold values from -16 to 16
- weight: bfloat16 [1024, 1024], P('feat', 'dom'), may hold values from -0.1875 to 0.1875
- bias: float32 [1024], P('feat'), may hold values from -3 to 3
- tile_values: bfloat16 [8192, 128, 128], P('dom'), may hold values from 0 to 10, as said below
- tile_rows: int32 [8192], P('dom'), may hold values from 0 to 1
- tile_cols: int32 [8192], P('dom'), may hold values from 0 to 127
- tile_live: int32 [64], P('dom'), may hold values from 0 to 128, as said below
- cotangent: bfloat16 [16384, 1024], P('dom', 'feat'), may hold values from -6 to 6
Outputs:
- output: bfloat16 [16384, 1024], P('dom', 'feat')
- feats_grad: bfloat16 [16384, 1024], P('dom', 'feat')
- weight_grad: float32 [1024, 1024], P('feat', 'dom')
- bias_grad: float32 [1024], P('feat')
Inputs may be any that keep to these rules, and one draw needn't show every extreme that they name: `tile_live`: device d and device d + 32 have at most 128 live slots together. Live slots are a device's first ones. `tile_values`: nonnegative edge weights.
All inputs are finite; a program needn't handle non-finite values.
Results may differ from a plain program's by a relative error of at most 0.0061.
Values may be sent and summed in bfloat16 or wider, within the bound.
No kernel may reach another device: no remote copies, remote signals or barrier semaphores. Data moves between devices by JAX's collectives and lax.ppermute only.
A program may use at most 128 MiB of HBM per device.

v0:
```python
import functools

import jax
import jax.numpy as jnp
from jax import lax
from jax.experimental import pallas as pl
from jax.experimental.pallas import tpu as pltpu
from jax.sharding import PartitionSpec as P

F32 = jnp.float32
BF16 = jnp.bfloat16
NZ, NX, NY = 8, 4, 4
BLK = 128
SLOTS = 128
WIDTH = 256
NODES = 2 * BLK
W_ROWS = 16
ROWS = NODES + W_ROWS
UNROLL = 8
FETCH = 16
BIAS_ROWS = 16
SUM_ROWS = 4 * ROWS + BIAS_ROWS
MIB = 1 << 20
VMEM = 54 * MIB

LOW, HIGH, ACROSS = (0, 1, 7, 2), (3, 4, 6, 5), (0, 1, 3, 2)
GATHER_0 = tuple(
    tuple(k * NZ + j for j in group)
    for k, group in ((0, LOW), (1, LOW), (3, LOW), (2, LOW), (3, HIGH), (1, HIGH), (2, HIGH), (0, HIGH))
)
GATHER_1 = tuple(tuple(k * NZ + j for k in ACROSS) for j in (0, 1, 7, 2, 6, 3, 5)) + (
    None,
    tuple(k * NZ + 4 for k in ACROSS[:2]),
    tuple(k * NZ + 4 for k in ACROSS[2:]),
)
FORWARD_CHUNKS = ((0, 1, 2), (3, 4, 7), (5, 6), (8, 9))
SCATTER = (
    (
        (None, tuple((dx, 4) for dx in ACROSS)),
        (tuple((2, dz) for dz in HIGH), None),
        (tuple((3, dz) for dz in HIGH), None),
    ),
    (
        (None, tuple((dx, 3) for dx in ACROSS)),
        (None, tuple((dx, 5) for dx in ACROSS)),
        (tuple((1, dz) for dz in HIGH), tuple((dx, 2) for dx in ACROSS)),
        (tuple((2, dz) for dz in LOW), tuple((dx, 6) for dx in ACROSS)),
        (tuple((1, dz) for dz in LOW), tuple((dx, 1) for dx in ACROSS)),
        (tuple((3, dz) for dz in LOW), tuple((dx, 7) for dx in ACROSS)),
        (tuple((0, dz) for dz in HIGH), None),
        (tuple((0, dz) for dz in LOW), tuple((dx, 0) for dx in ACROSS)),
    ),
)


def shift(value, core_0=None, core_1=None):
    pairs = []
    for z in range(NZ):
        for x in range(NX):
            for core, step in enumerate((core_0, core_1)):
                if step is not None:
                    target = ((z + step[0]) % NZ * NX + (x + step[1]) % NX) * 2 + core
                    pairs.append(((z * NX + x) * 2 + core, target))
    return lax.ppermute(value, "dom", pairs)


Z_UP, Z_DOWN, Z_UP_2, Z_DOWN_2 = (1, 0), (-1, 0), (2, 0), (-2, 0)
X_UP, X_DOWN, X_TWO = (0, 1), (0, -1), (0, 2)


def swap(value, bit):
    return lax.ppermute(value, "dom", [(i, i ^ bit) for i in range(NZ * NX * 2)])


def y_shift(value, dy):
    return lax.ppermute(value, "feat", [(y, (y + dy) % NY) for y in range(NY)])


def smem():
    return pl.BlockSpec(memory_space=pltpu.SMEM)


def vmem():
    return pl.BlockSpec(memory_space=pltpu.VMEM)


def anywhere():
    return pl.BlockSpec(memory_space=pl.ANY)


def list_kernel(place, own, sib, lists):
    core, x, z = place[0], place[1], place[2]
    wide = (1, 2 * SLOTS)
    column = jnp.concatenate([own[1:2], sib[1:2]], axis=1)
    row = jnp.concatenate([own[0:1], sib[0:1] + 2], axis=1)
    slot = lax.broadcasted_iota(jnp.int32, wide, 1)
    live = slot < jnp.where(slot < SLOTS, place[4], SLOTS + place[5])
    owner = column >> 1
    chip = owner >> 1
    k = (x - (chip & (NX - 1))) & (NX - 1)
    j = (z - (chip >> 2)) & (NZ - 1)
    spot = (k * NZ + j) * 2 + (column & 1)
    mine = live & ((owner & 1) == core)
    high, back = (j >= 3) & (j <= 6), (j >= 2) & (j <= 5)
    on_0 = jnp.where(high, jnp.where((k == 1) | (k == 2), 2, 1), jnp.where(k == 2, 1, 0))
    on_1 = jnp.where(j == 4, 3, jnp.where((j == 3) | (j == 5), 2, jnp.where((j == 2) | (j == 6), 1, 0)))
    forward_call = jnp.where(core == 0, on_0, on_1)
    backward_call = jnp.where(core == 0, jnp.where(back & ((k == 1) | (k == 2)), 0, 1), jnp.where(j == 4, 0, 1))
    square = (2 * SLOTS, 2 * SLOTS)
    first = lax.broadcasted_iota(jnp.int32, square, 0)
    second = lax.broadcasted_iota(jnp.int32, square, 1)
    up_to = jnp.where(first <= second, 1.0, 0.0).astype(BF16)
    group_of = lax.broadcasted_iota(jnp.int32, (16, 2 * SLOTS), 0)
    lane = lax.broadcasted_iota(jnp.int32, (16, 2 * SLOTS), 1)
    before = jnp.where(
        lax.broadcasted_iota(jnp.int32, (16, 16), 1) < lax.broadcasted_iota(jnp.int32, (16, 16), 0), 1.0, 0.0
    ).astype(BF16)
    values = jnp.concatenate([slot, spot], axis=0).astype(F32)
    values = jnp.concatenate([values, jnp.zeros((14, 2 * SLOTS), F32)], axis=0).astype(BF16)
    lists[...] = jnp.zeros_like(lists)
    for at, call in ((0, forward_call), (3, backward_call)):
        group = jnp.where(mine, call * 4 + row, -1)
        member = jnp.where(group_of == group, 1.0, 0.0)
        rank = jnp.dot(member.astype(BF16), up_to, preferred_element_type=F32)
        counts = jnp.sum(member, axis=1, keepdims=True)
        earlier = jnp.dot(before, member.astype(BF16), preferred_element_type=F32)
        starts = jnp.sum(earlier, axis=1, keepdims=True)
        goal = jnp.sum(member * (starts + rank), axis=0, keepdims=True).astype(jnp.int32) - 1
        moved = jnp.where(first == goal, 1.0, 0.0).astype(BF16)
        ordered = lax.dot_general(values, moved, (((1,), (1,)), ((), ())), preferred_element_type=F32)
        lists[at : at + 1, :] = jnp.sum(jnp.where(group_of == lane, counts, 0.0), axis=0, keepdims=True).astype(jnp.int32)
        lists[at + 1 : at + 2, :] = jnp.sum(jnp.where(group_of == lane, starts, 0.0), axis=0, keepdims=True).astype(jnp.int32)
        lists[at + 2 : at + 3, :] = (ordered[0:1] * 64.0 + ordered[1:2]).astype(jnp.int32)
    told = jnp.zeros(wide, jnp.int32)
    for i in range(6):
        told = jnp.where(slot == i, place[i], told)
    lists[6:7, :] = told


def make_lists(place, own, sib):
    return pl.pallas_call(
        list_kernel,
        out_shape=jax.ShapeDtypeStruct((8, 2 * SLOTS), jnp.int32),
        in_specs=[smem(), vmem(), vmem()],
        out_specs=vmem(),
    )(place, own, sib)


def place_of(lists):
    return [lists[6, i] for i in range(4)]


def copy_each(copies, action):
    for condition, copy in copies:
        call = getattr(copy, action)
        if condition is None:
            call()
        else:
            pl.when(condition)(call)


class Tiles:
    def __init__(self, lists, at, call, every, own, sib, held, sem):
        self.lists, self.at, self.call, self.every = lists, at, call, every
        self.own, self.sib, self.held, self.sem = own, sib, held, sem
        self.begin = lists[at + 1, call * 4]
        self.end = lists[at + 1, call * 4 + 3] + lists[at, call * 4 + 3]

    def bulk(self):
        copies = []
        for which, source in enumerate((self.own, self.sib)):
            for step in range(SLOTS // FETCH):
                first = step * FETCH
                copy = pltpu.make_async_copy(
                    source.at[pl.ds(first, FETCH)],
                    self.held.at[pl.ds(which * SLOTS + first, FETCH)],
                    self.sem.at[which * (SLOTS // FETCH) + step],
                )
                copies.append((first < self.lists[6, 4 + which], copy))
        return copies

    def each(self, action):
        def step(p, carry):
            slot = self.lists[self.at + 2, p] >> 6
            goal = self.held.at[p]

            @pl.when(slot < SLOTS)
            def _():
                getattr(pltpu.make_async_copy(self.own.at[jnp.minimum(slot, SLOTS - 1)], goal, self.sem.at[0]), action)()

            @pl.when(slot >= SLOTS)
            def _():
                getattr(pltpu.make_async_copy(self.sib.at[jnp.maximum(slot - SLOTS, 0)], goal, self.sem.at[0]), action)()

            return carry

        lax.fori_loop(self.begin, self.end, step, 0)

    def start(self):
        if self.every:
            copy_each(self.bulk(), "start")
        else:
            self.each("start")
        self.held[2 * SLOTS] = jnp.zeros((BLK, BLK), BF16)

    def wait(self):
        if self.every:
            copy_each(self.bulk(), "wait")
        else:
            self.each("wait")

    def rows(self):
        for row in range(4):
            group = self.call * 4 + row
            number, first = self.lists[self.at, group], self.lists[self.at + 1, group]

            def pick(it, number=number, first=first):
                lefts, spots = [], []
                for u in range(UNROLL):
                    p = it * UNROLL + u
                    entry = self.lists[self.at + 2, first + jnp.minimum(p, number - 1)]
                    place = entry >> 6 if self.every else first + p
                    lefts.append(self.held[jnp.where(p < number, place, 2 * SLOTS)])
                    spots.append(entry & 63)
                return jnp.concatenate(lefts, axis=1), spots

            yield row, lax.div(number + (UNROLL - 1), UNROLL), pick


def forward_kernel(call, lists, own, sib, *rest):
    chosen = FORWARD_CHUNKS[call]
    chunks, rest = rest[: len(chosen)], rest[len(chosen) :]
    if call:
        own_before, sib_before, weight_before, *rest = rest
    own_sums, sib_sums, weight_out, blocks, held, sem, tile_sem = rest
    core, x, z, y = place_of(lists)
    tiles = Tiles(lists, 0, call, False, own, sib, held, tile_sem)
    tiles.start()
    copies, arrived = [], []
    for n, chunk in zip(chosen, chunks):
        condition = None if n < 7 else core == (0 if n == 7 else 1)
        for i in range(chunk.shape[0]):
            if n < 7:
                spot = jnp.where(core == 0, GATHER_0[n][i], GATHER_1[n][i])
            else:
                spot = GATHER_0[n][i] if n == 7 else GATHER_1[n][i]
            copies.append((condition, pltpu.make_async_copy(chunk.at[i], blocks.at[spot], sem.at[len(copies)])))
            arrived.append((condition, spot))
    copy_each(copies, "start")
    copy_each(copies, "wait")
    tiles.wait()
    for row, steps, pick in tiles.rows():

        def step(it, total):
            left, spots = pick(it)
            rights = []
            for spot in spots:
                first = pl.multiple_of((spot & 1) * BLK, BLK)
                rights.append(blocks[spot >> 1, pl.ds(first, BLK), :])
            return total + jnp.dot(left, jnp.concatenate(rights, axis=0), preferred_element_type=F32)

        sums, at = (own_sums, row) if row < 2 else (sib_sums, row - 2)
        before = jnp.zeros((BLK, WIDTH), F32)
        if call:
            before = own_before[at] if row < 2 else sib_before[at]
        sums[at] = lax.fori_loop(0, steps, step, before)
    if call:
        weight_out[...] = weight_before[...]
    for condition, spot in arrived:

        def keep(spot=spot):
            column = (x - (spot >> 3)) & (NX - 1)
            level = (z - spot) & (NZ - 1)
            part = ((level >> 1) - y) & (NY - 1)
            weight_out[part, (level & 1) * NX + column] = blocks[spot, NODES:ROWS, :]

        if condition is None:
            keep()
        else:
            pl.when(condition)(keep)


def forward(call, lists, own, sib, chunks, before):
    chosen = [chunks[n] for n in FORWARD_CHUNKS[call]]
    return pl.pallas_call(
        functools.partial(forward_kernel, call),
        out_shape=(
            jax.ShapeDtypeStruct((2, BLK, WIDTH), F32),
            jax.ShapeDtypeStruct((2, BLK, WIDTH), F32),
            jax.ShapeDtypeStruct((NY, 2 * NX, W_ROWS, WIDTH), BF16),
        ),
        in_specs=[smem()] + [anywhere()] * (2 + len(chosen)) + [vmem()] * len(before),
        out_specs=(vmem(),) * 3,
        scratch_shapes=[
            pltpu.VMEM((NX * NZ, ROWS, WIDTH), BF16),
            pltpu.VMEM((2 * SLOTS + 1, BLK, BLK), BF16),
            pltpu.SemaphoreType.DMA((32,)),
            pltpu.SemaphoreType.DMA((2 * SLOTS // FETCH,)),
        ],
        compiler_params=pltpu.CompilerParams(vmem_limit_bytes=VMEM),
        cost_estimate=pl.CostEstimate(
            flops=2 * BLK * BLK * WIDTH * len(chosen) * 16, bytes_accessed=len(chosen) * MIB, transcendentals=0
        ),
    )(lists, own, sib, *chosen, *before)


def backward_kernel(call, lists, own, sib, scaled, other_scaled, weight_sums, chip_bias, *rest):
    chunks = SCATTER[call]
    outs, rest = rest[: len(chunks)], rest[len(chunks) :]
    total, held, tile_sem = rest
    core, x, z, y = place_of(lists)
    tiles = Tiles(lists, 3, call, call == 1, own, sib, held, tile_sem)
    tiles.start()

    def each_chunk(action):
        for out, chunk in zip(outs, chunks):
            if None in chunk:
                side = 1 if chunk[0] is None else 0

                @pl.when(core == side)
                def _(out=out, places=chunk[side]):
                    action(out, places)
            else:
                action(out, [[jnp.where(core == 0, p, q) for p, q in zip(*pair)] for pair in zip(*chunk)])

    def spot_of(dx, dz):
        return ((0 - dx) & (NX - 1)) * NZ + ((0 - dz) & (NZ - 1))

    def clear(out, places):
        for dx, dz in places:
            spot = spot_of(dx, dz)
            total[spot * 2] = jnp.zeros((BLK, WIDTH), F32)
            total[spot * 2 + 1] = jnp.zeros((BLK, WIDTH), F32)

    def emit(out, places):
        for i, (dx, dz) in enumerate(places):
            spot = spot_of(dx, dz)
            first = i * ROWS
            out[first : first + BLK, :] = total[spot * 2].astype(BF16)
            out[first + BLK : first + NODES, :] = total[spot * 2 + 1].astype(BF16)
            column = (x + dx) & (NX - 1)
            level = (z + dz) & (NZ - 1)
            part = ((level >> 1) - y) & (NY - 1)
            out[first + NODES : first + ROWS, :] = weight_sums[part, (level & 1) * NX + column]
        out[4 * ROWS : SUM_ROWS, :] = bias_block(rows_of(chip_bias[...]) if call == 0 else [])

    each_chunk(clear)
    tiles.wait()
    for row, steps, pick in tiles.rows():
        right = scaled[row] if row < 2 else other_scaled[row - 2]

        def step(it, carry):
            left, spots = pick(it)
            terms = lax.dot_general(left, right, (((0,), (0,)), ((), ())), preferred_element_type=F32)
            for u, spot in enumerate(spots):
                total[spot] += terms[u * BLK : (u + 1) * BLK]
            return carry

        lax.fori_loop(0, steps, step, 0)
    each_chunk(emit)


def backward(call, lists, own, sib, scaled, other_scaled, weight_sums, chip_bias):
    shapes = []
    for _ in SCATTER[call]:
        shapes.append(jax.ShapeDtypeStruct((SUM_ROWS, WIDTH), BF16))
    return pl.pallas_call(
        functools.partial(backward_kernel, call),
        out_shape=tuple(shapes),
        in_specs=[smem()] + [anywhere()] * 2 + [vmem()] * 4,
        out_specs=(vmem(),) * len(shapes),
        scratch_shapes=[
            pltpu.VMEM((2 * NX * NZ, BLK, WIDTH), F32),
            pltpu.VMEM((2 * SLOTS + 1, BLK, BLK), BF16),
            pltpu.SemaphoreType.DMA((2 * SLOTS // FETCH,)),
        ],
        compiler_params=pltpu.CompilerParams(vmem_limit_bytes=VMEM),
        cost_estimate=pl.CostEstimate(
            flops=2 * BLK * BLK * WIDTH * len(shapes) * 16, bytes_accessed=len(shapes) * MIB, transcendentals=0
        ),
    )(lists, own, sib, scaled, other_scaled, weight_sums, chip_bias)


def gather(block, core, lists, other_tiles, degree, call):
    p1 = shift(block, Z_UP, X_UP)
    p2 = shift(block, Z_DOWN, X_DOWN)
    p3 = shift(block, Z_UP_2, X_TWO)
    low, other_tiles = lax.optimization_barrier((jnp.stack([block, p1, p2, p3]), other_tiles))
    c1 = shift(low, X_UP, Z_UP)
    c2 = shift(low, X_DOWN, Z_DOWN)
    pa = shift(jnp.stack([low[1], low[3]]), Z_UP_2)
    pb = shift(jnp.stack([low[0], low[2]]), Z_DOWN_2)
    c1, c2, pa, pb, lists, degree = lax.optimization_barrier((c1, c2, pa, pb, lists, degree))
    high = jnp.concatenate([pa, pb], axis=0)
    early = lists, other_tiles
    c3 = shift(c1, X_UP, Z_UP)
    c4 = shift(jnp.where(core == 0, high, c2), X_DOWN, Z_DOWN)
    chunks = [low, c1, c2]
    sums = call(0, early, chunks, ())
    c3, c4, sums = lax.optimization_barrier((c3, c4, sums))
    chunks += [c3, c4, None, None, high]
    sums = call(1, early, chunks, sums)
    c5 = shift(jnp.where(core == 0, high, c3), X_UP, Z_UP)
    c6 = shift(c4, X_DOWN, Z_DOWN)
    c5, c6, sums = lax.optimization_barrier((c5, c6, sums))
    chunks[5:7] = c5, c6
    chunks += [shift(c5[:2], None, Z_UP), shift(c6[2:], None, Z_DOWN)]
    return degree, call(3, early, chunks, call(2, early, chunks, sums))


def add(*values):
    total = values[0].astype(F32)
    for value in values[1:]:
        total = total + value.astype(F32)
    return total


def rows_of(value):
    high = value.astype(BF16)
    middle = (value - high.astype(F32)).astype(BF16)
    low = (value - high.astype(F32) - middle.astype(F32)).astype(BF16)
    return [high.astype(F32), middle.astype(F32), low.astype(F32)]


def bias_block(rows):
    used = sum(row.shape[0] for row in rows)
    rows = rows + [jnp.zeros((BIAS_ROWS - used, WIDTH), F32)]
    return jnp.concatenate(rows, axis=0).astype(BF16)


def joined(block, first=0):
    rows = block.astype(F32)
    return rows[first : first + 1] + rows[first + 1 : first + 2] + rows[first + 2 : first + 3]


def in_order(values, place, held):
    count = len(values)
    for k, value in enumerate(values):
        held[k : k + 1, :] = value
    total = held[pl.ds(place & (count - 1), 1), :]
    for i in range(1, count):
        total = total + held[pl.ds((place - i) & (count - 1), 1), :]
    return total


def block_sum(i, *chunks):
    total = chunks[0][i * ROWS : (i + 1) * ROWS, :].astype(F32)
    for chunk in chunks[1:]:
        total = total + chunk[i * ROWS : (i + 1) * ROWS, :].astype(F32)
    return total


def tail_of(chunk):
    return chunk[4 * ROWS : SUM_ROWS, :]


def pair_kernel(lists, chip_bias, h0, ja1, ja2, jb1, pair_a, pair_b, line_bias, held):
    line = in_order([chip_bias[...], joined(tail_of(ja1)), joined(tail_of(jb1)), joined(tail_of(ja2))], lists[6, 1], held)
    line_bias[...] = line
    rows = bias_block(rows_of(line))
    for pair, first in ((pair_a, 0), (pair_b, 2)):
        for i in range(2):
            pair[i * ROWS : (i + 1) * ROWS, :] = block_sum(first + i, h0, jb1, ja2).astype(BF16)
        pair[2 * ROWS : 2 * ROWS + BIAS_ROWS, :] = rows


def message_kernel(line_bias, h1, jc1, jc2, ra, rb, m1, m2, m3, rest):
    own = rows_of(line_bias[...])
    rest[...] = block_sum(0, h1, jc1, jc2) + block_sum(0, rb)
    relayed = [chunk[2 * ROWS : 2 * ROWS + BIAS_ROWS, :].astype(F32)[0:3] for chunk in (ra, rb)]
    m1[0:ROWS, :] = (block_sum(1, h1, jc1, jc2) + block_sum(0, ra)).astype(BF16)
    m1[ROWS:, :] = bias_block(own + [relayed[0]])
    m2[0:ROWS, :] = (block_sum(2, h1, jc1, jc2) + block_sum(1, rb)).astype(BF16)
    m2[ROWS:, :] = bias_block(own + [relayed[1]])
    m3[0:ROWS, :] = (block_sum(3, h1, jc1, jc2) + block_sum(1, ra)).astype(BF16)
    m3[ROWS:, :] = bias_block(own + [relayed[0]])


def bias_kernel(lists, line_bias, r1, r2, r3, rb, bias, held):
    t1, t2, t3 = (chunk[ROWS:, :] for chunk in (r1, r2, r3))
    tb = rb[2 * ROWS :, :]
    values = [line_bias[...], joined(t1), joined(t3), joined(t1, 3), joined(t3, 3), joined(t2, 3), joined(tb), joined(t2)]
    bias[...] = in_order(values, lists[6, 2], held)


def last_kernel(rest, r1, r2, r3, scaled, feats_grad, weight_grad):
    total = rest[...] + block_sum(0, r1, r2, r3)
    feats_grad[...] = (scaled[...].astype(F32) + total[0:NODES]).astype(BF16)
    weight_grad[...] = total[NODES:ROWS]


def small_call(kernel, shapes, lists, operands, scratch):
    first = [] if lists is None else [lists]
    return pl.pallas_call(
        kernel,
        out_shape=tuple(jax.ShapeDtypeStruct(shape, dtype) for shape, dtype in shapes),
        in_specs=[smem()] * len(first) + [vmem()] * len(operands),
        out_specs=(vmem(),) * len(shapes),
        scratch_shapes=[pltpu.VMEM((8, WIDTH), F32)] * scratch,
        compiler_params=pltpu.CompilerParams(vmem_limit_bytes=16 * MIB),
    )(*first, *operands)


def scatter(parts, weight_sums, core, lists, chip_bias, scaled):
    first_up, x1, x2 = parts(0, weight_sums)
    zero = jnp.zeros((), BF16)
    j0 = shift(first_up, None, Z_UP)
    y1, y2, b1, b2, q1, q2, h0, h1 = parts(1, weight_sums)
    ja1 = shift(jnp.where(core == 0, x1, add(y1, j0).astype(BF16)), X_UP, Z_UP)
    ja2 = shift(jnp.where(core == 0, x2, y2), X_DOWN, Z_DOWN)
    ja1, ja2 = lax.optimization_barrier((ja1, ja2))
    jb1 = shift(add(b1, ja1).astype(BF16), X_UP, Z_UP)
    jb2 = shift(add(b2, jnp.where(core == 0, zero, ja2)).astype(BF16), X_DOWN, Z_DOWN)
    jb1, jb2 = lax.optimization_barrier((jb1, jb2))
    wide = (2 * ROWS + BIAS_ROWS, WIDTH)
    pair_a, pair_b, line_bias = small_call(
        pair_kernel, ((wide, BF16), (wide, BF16), ((1, WIDTH), F32)), lists, (chip_bias, h0, ja1, ja2, jb1), 1
    )
    jc1 = shift(add(q1, jnp.where(core == 0, zero, jb1)).astype(BF16), X_UP, Z_UP)
    jc2 = shift(add(q2, jb2).astype(BF16), X_DOWN, Z_DOWN)
    ra = shift(pair_a, Z_UP_2)
    rb = shift(pair_b, Z_DOWN_2)
    jc1, jc2, ra, rb = lax.optimization_barrier((jc1, jc2, ra, rb))
    size = (ROWS + BIAS_ROWS, WIDTH)
    m1, m2, m3, rest = small_call(
        message_kernel,
        ((size, BF16), (size, BF16), (size, BF16), ((ROWS, WIDTH), F32)),
        None,
        (line_bias, h1, jc1, jc2, ra, rb),
        0,
    )
    r1 = shift(m1, Z_UP, X_UP)
    r2 = shift(m2, Z_DOWN, X_DOWN)
    r3 = shift(m3, Z_UP_2, X_TWO)
    (bias,) = small_call(bias_kernel, (((1, WIDTH), F32),), lists, (line_bias, r1, r2, r3, rb), 1)
    from_core_0 = lax.ppermute(bias, "dom", [(i, i + 1) for i in range(0, NZ * NX * 2, 2)])
    feats_grad, weight_grad = small_call(
        last_kernel, (((NODES, WIDTH), BF16), ((W_ROWS, WIDTH), F32)), None, (rest, r1, r2, r3, scaled), 0
    )
    return feats_grad, weight_grad, jnp.where(core == 0, bias, from_core_0)


def silu_parts(hidden):
    gate_value = jax.nn.sigmoid(hidden)
    return (hidden * gate_value, gate_value * (1.0 + hidden * (1.0 - gate_value)))


def on_device(feats, weight, bias, tile_values, tile_rows, tile_cols, tile_live, cotangent):
    dom = lax.axis_index("dom")
    y = lax.axis_index("feat")
    core = dom % 2
    x = (dom // 2) % NX
    z = dom // (2 * NX)

    meta = jnp.stack([tile_rows, tile_cols, jnp.broadcast_to(tile_live, (SLOTS,))])
    other_meta = swap(meta, 1)
    place = jnp.stack([core, x, z, y, tile_live[0], other_meta[2, 0]]).astype(jnp.int32)
    lists = make_lists(place, meta, other_meta)

    own_live = jnp.arange(SLOTS, dtype=jnp.int32) < tile_live[0]
    row_sums = jnp.sum(tile_values, axis=2, dtype=F32)
    degree = 1.0 + jnp.concatenate(
        [
            jnp.sum(jnp.where((own_live & (tile_rows == row))[:, None], row_sums, 0.0), axis=0)
            for row in range(2)
        ]
    ).reshape(NODES, 1)

    other_tiles = swap(tile_values, 1)
    degree, (sums, other_sums, weight_lane) = gather(
        jnp.concatenate([feats, weight.T], axis=0),
        core,
        lists,
        other_tiles,
        degree,
        lambda call, early, chunks, before: forward(call, early[0], tile_values, early[1], chunks, before),
    )
    neighbour_sum = (sums + swap(other_sums, 1)).reshape(NODES, WIDTH)
    weight_other = swap(weight_lane, 1)
    mixed = ((feats.astype(F32) + neighbour_sum) / degree).astype(BF16)

    first = jnp.where(core == 0, weight_lane, weight_other)
    second = jnp.where(core == 0, weight_other, weight_lane)
    weight_t = jnp.stack([first, second], axis=2).reshape(NY, WIDTH, WIDTH)

    def hidden_part(dy):
        return lax.dot_general(mixed, weight_t[dy], (((1,), (1,)), ((), ())), preferred_element_type=F32)

    hidden = add(
        hidden_part(0),
        y_shift(hidden_part(1).astype(BF16), 1),
        y_shift(hidden_part(2).astype(BF16), 2),
        y_shift(hidden_part(3).astype(BF16), 3),
    ) + bias
    activated, slope = silu_parts(hidden)
    output = activated.astype(BF16)
    dz_full = cotangent.astype(F32) * slope
    dz_own = dz_full.astype(BF16)
    dz_parts = [dz_own] + [y_shift(dz_own, NY - dy) for dy in range(1, NY)]

    dmixed = sum(jnp.dot(dz_parts[dy], weight_t[dy], preferred_element_type=F32) for dy in range(NY))
    scaled = (dmixed / degree).astype(BF16)
    scaled_blocks = [value.reshape(2, BLK, WIDTH) for value in (scaled, swap(scaled, 1))]

    weight_part = jnp.stack(
        [
            lax.dot_general(dz_parts[dy], mixed, (((0,), (0,)), ((), ())), preferred_element_type=F32)
            for dy in range(NY)
        ]
    ).reshape(NY, 2 * NX, 2, W_ROWS, WIDTH)
    mine = jnp.where(core == 0, weight_part[:, :, 0], weight_part[:, :, 1])
    others = jnp.where(core == 0, weight_part[:, :, 1], weight_part[:, :, 0])
    bias_part = jnp.sum(dz_full, axis=0, keepdims=True)
    sent = jnp.concatenate([others.reshape(-1, WIDTH), jnp.pad(bias_part, ((0, 7), (0, 0)))], axis=0)
    got = swap(sent, 1)
    weight_sums = (mine + got[:-8].reshape(mine.shape)).astype(BF16)

    chip_bias = bias_part + got[-8:-7]

    def parts(call, weight_sums):
        return backward(call, lists, tile_values, other_tiles, *scaled_blocks, weight_sums, chip_bias)

    feats_grad, weight_sum, bias_grad = scatter(parts, weight_sums, core, lists, chip_bias, scaled)
    return (output, feats_grad, weight_sum.T, bias_grad.reshape(WIDTH))


def solution(mesh):
    return jax.shard_map(
        on_device,
        mesh=mesh,
        in_specs=(
            P("dom", "feat"),
            P("feat", "dom"),
            P("feat"),
            P("dom", None, None),
            P("dom"),
            P("dom"),
            P("dom"),
            P("dom", "feat"),
        ),
        out_specs=(P("dom", "feat"), P("dom", "feat"), P("feat", "dom"), P("feat")),
        check_vma=False,
    )
```

profile of v0, /device:TPU:1, one launch (start us, length us, event | category | flops | bytes accessed | tf_op | source)
XLA Modules:
  0.0 183.0 jit_solution(17893467753985584749)
XLA Ops:
  0.6 3.3 %collective-permute-start.3 = (bf16[128,128,128]{2,1,0:T(8,128)(2,1)}, bf16[128,128,128]{2,1,0:T(8,128)(2,1)}, u32[]{:S(2)}, u32[]{:S(2)}) collective-permute-start(bf16[128,128,128]{2,1,0:T(8,128)(2,1)} %own.11), channel_id=1, source_target_pairs={{0,4},{4,0},{8,12},{12,8},{16,20},{20,16},{24,28},{28,24},{32,36},... | collective-permute-start | bytes 12582920 | tf_op jit(solution)/shard_map/ppermute | solution.py:72
  4.0 0.9 fusion.11
  4.9 0.8 collective-permute-start.1
  5.7 0.7 collective-permute-start
  6.4 1.0 collective-permute-start.2
  8.2 0.7 add_add_fusion.1.own
  8.9 1.7 collective-permute-start.8
  10.6 3.4 %convert_reduce_fusion = f32[128,128]{1,0:T(8,128)S(1)} fusion(bf16[128,128,128]{2,1,0:T(8,128)(2,1)} %own.11), kind=kLoop, calls=%fused_computation | loop fusion | flops 4177920 | bytes 4259840 | tf_op jit(solution)/shard_map/reduce_sum | solution.py:561
  14.2 4.1 %collective-permute-start.5 = (bf16[4,272,256]{2,1,0:T(8,128)(2,1)S(1)}, bf16[4,272,256]{2,1,0:T(8,128)(2,1)S(1)}, u32[]{:S(2)}, u32[]{:S(2)}) collective-permute-start(bf16[4,272,256]{2,1,0:T(8,128)(2,1)S(1)} %pad_maximum_fusion.1.rest_0_), channel_id=1, source_target_pairs={{0,24},{4,228},{8,0},{12,236},{16,8},{20,244},{24,16},{28,252},{32... | collective-permute-start | bytes 1671176 | tf_op jit(solution)/shard_map/ppermute | solution.py:64
  20.5 1.2 stack.83.place
  21.7 1.8 shard_map.114.lists
  23.6 1.2 collective-permute-done.5.rest_2_
  24.8 6.8 %collective-permute-done.4.rest_1_ = bf16[4,272,256]{2,1,0:T(8,128)(2,1)S(1)} collective-permute-done((bf16[4,272,256]{2,1,0:T(8,128)(2,1)S(1)}, bf16[4,272,256]{2,1,0:T(8,128)(2,1)S(1)}, u32[]{:S(2)}, u32[]{:S(2)}) %collective-permute-start.4) | collective-permute-done | bytes 557088 | tf_op jit(solution)/shard_map/ppermute | solution.py:64
  32.4 0.9 collective-permute-start.9
  33.2 4.5 %shard_map.115 = (f32[2,128,256]{2,1,0:T(8,128)}, f32[2,128,256]{2,1,0:T(8,128)}, bf16[4,8,16,256]{3,2,1,0:T(8,128)(2,1)}) custom-call(s32[8,256]{1,0:T(8,128)} %shard_map.114.lists, bf16[128,128,128]{2,1,0:T(8,128)(2,1)} %own.11, bf16[128,128,128]{2,1,0:T(8,128)(2,1)} %collective-permute-done.3.sib, bf16[4,272,256]{2,1,0:T(8,128)(2,1)} %copy-done.7, ...), custom_call_target="tpu_custom_call" | custom-call | flops 402653184 | bytes 3145728 | tf_op jit(solution)/shard_map/pallas_call | solution.py:285
  37.8 4.3 %collective-permute-done.10.rest_1_ = bf16[4,272,256]{2,1,0:T(8,128)(2,1)S(1)} collective-permute-done((bf16[4,272,256]{2,1,0:T(8,128)(2,1)S(1)}, bf16[4,272,256]{2,1,0:T(8,128)(2,1)S(1)}, u32[]{:S(2)}, u32[]{:S(2)}) %collective-permute-start.10) | collective-permute-done | bytes 557088 | tf_op jit(solution)/shard_map/ppermute | solution.py:64
  42.2 2.7 %collective-permute-start.12 = (bf16[4,272,256]{2,1,0:T(8,128)(2,1)S(1)}, bf16[4,272,256]{2,1,0:T(8,128)(2,1)S(1)}, u32[]{:S(2)}, u32[]{:S(2)}) collective-permute-start(bf16[4,272,256]{2,1,0:T(8,128)(2,1)S(1)} %collective-permute-done.10.rest_1_), channel_id=1, source_target_pairs={{0,24},{4,228},{8,0},{12,236},{16,8},{20,244},{24,16},{28,252},{32... | collective-permute-start | bytes 1671176 | tf_op jit(solution)/shard_map/ppermute | solution.py:64
  44.9 5.5 %shard_map.116 = (f32[2,128,256]{2,1,0:T(8,128)}, f32[2,128,256]{2,1,0:T(8,128)}, bf16[4,8,16,256]{3,2,1,0:T(8,128)(2,1)}) custom-call(s32[8,256]{1,0:T(8,128)} %shard_map.114.lists, bf16[128,128,128]{2,1,0:T(8,128)(2,1)} %own.11, bf16[128,128,128]{2,1,0:T(8,128)(2,1)} %collective-permute-done.3.sib, bf16[4,272,256]{2,1,0:T(8,128)(2,1)} %copy-done.9, ...), custom_call_target="tpu_custom_call" | custom-call | flops 402653184 | bytes 3145728 | tf_op jit(solution)/shard_map/pallas_call | solution.py:285
  50.4 1.7 collective-permute-done.11.rest_0_
  52.2 2.1 %collective-permute-start.13 = (bf16[2,272,256]{2,1,0:T(8,128)(2,1)S(1)}, bf16[2,272,256]{2,1,0:T(8,128)(2,1)S(1)}, u32[]{:S(2)}, u32[]{:S(2)}) collective-permute-start(bf16[2,272,256]{2,1,0:T(8,128)(2,1)S(1)} %slice.60), channel_id=1, source_target_pairs={{4,36},{12,44},{20,52},{28,60},{36,68},{44,76},{52,84},{60,92},{68... | collective-permute-start | bytes 835592 | tf_op jit(solution)/shard_map/ppermute | solution.py:64
  54.3 4.6 %collective-permute-start.14 = (bf16[2,272,256]{2,1,0:T(8,128)(2,1)S(1)}, bf16[2,272,256]{2,1,0:T(8,128)(2,1)S(1)}, u32[]{:S(2)}, u32[]{:S(2)}) collective-permute-start(bf16[2,272,256]{2,1,0:T(8,128)(2,1)S(1)} %slice.61), channel_id=1, source_target_pairs={{4,228},{12,236},{20,244},{28,252},{36,4},{44,12},{52,20},{60,28},... | collective-permute-start | bytes 835592 | tf_op jit(solution)/shard_map/ppermute | solution.py:64
  58.9 5.9 %shard_map.117 = (f32[2,128,256]{2,1,0:T(8,128)}, f32[2,128,256]{2,1,0:T(8,128)}, bf16[4,8,16,256]{3,2,1,0:T(8,128)(2,1)}) custom-call(s32[8,256]{1,0:T(8,128)} %shard_map.114.lists, bf16[128,128,128]{2,1,0:T(8,128)(2,1)} %own.11, bf16[128,128,128]{2,1,0:T(8,128)(2,1)} %collective-permute-done.3.sib, bf16[4,272,256]{2,1,0:T(8,128)(2,1)} %copy-done.10, ...), custom_call_target="tpu_custom_call" | custom-call | flops 268435456 | bytes 2097152 | tf_op jit(solution)/shard_map/pallas_call | solution.py:285
  64.8 0.7 copy-done.23
  65.7 4.2 %shard_map.118 = (f32[2,128,256]{2,1,0:T(8,128)}, f32[2,128,256]{2,1,0:T(8,128)}, bf16[4,8,16,256]{3,2,1,0:T(8,128)(2,1)}) custom-call(s32[8,256]{1,0:T(8,128)} %shard_map.114.lists, bf16[128,128,128]{2,1,0:T(8,128)(2,1)} %own.11, bf16[128,128,128]{2,1,0:T(8,128)(2,1)} %collective-permute-done.3.sib, bf16[2,272,256]{2,1,0:T(8,128)(2,1)} %copy-done.23, ...), custom_call_target="tpu_custom_call" | custom-call | flops 268435456 | bytes 2097152 | tf_op jit(solution)/shard_map/pallas_call | solution.py:285
  69.9 4.5 %collective-permute-start.16 = (bf16[4,8,16,256]{3,2,1,0:T(8,128)(2,1)}, bf16[4,8,16,256]{3,2,1,0:T(8,128)(2,1)S(1)}, u32[]{:S(2)}, u32[]{:S(2)}) collective-permute-start(bf16[4,8,16,256]{3,2,1,0:T(8,128)(2,1)} %get-tuple-element.91), channel_id=1, source_target_pairs={{0,4},{4,0},{8,12},{12,8},{16,20},{20,16},{24,28},{28,24},{32,36},... | collective-permute-start | bytes 786440 | tf_op jit(solution)/shard_map/ppermute | solution.py:72
  74.5 1.3 collective-permute-done.16
  75.8 1.0 select_bitcast_fusion.1
  76.9 0.8 copy-done.25
  78.6 3.0 %collective-permute-start.18 = (bf16[256,256]{1,0:T(8,128)(2,1)S(1)}, bf16[256,256]{1,0:T(8,128)(2,1)S(1)}, u32[]{:S(2)}, u32[]{:S(2)}) collective-permute-start(bf16[256,256]{1,0:T(8,128)(2,1)S(1)} %convolution_convert_fusion.1), channel_id=1, source_target_pairs={{0,2},{1,3},{2,0},{3,1},{4,6},{5,7},{6,4},{7,5},{8,10},{9,11},{10,... | collective-permute-start | bytes 393224 | tf_op jit(solution)/shard_map/ppermute | solution.py:76
  81.6 0.8 collective-permute-start.19
  82.4 0.7 collective-permute-start.17
  83.3 1.6 collective-permute-done.18
  84.9 3.1 %collective-permute-done.19 = bf16[256,256]{1,0:T(8,128)(2,1)S(1)} collective-permute-done((bf16[256,256]{1,0:T(8,128)(2,1)S(1)}, bf16[256,256]{1,0:T(8,128)(2,1)S(1)}, u32[]{:S(2)}, u32[]{:S(2)}) %collective-permute-start.19) | collective-permute-done | bytes 131104 | tf_op jit(solution)/shard_map/ppermute | solution.py:76
  88.1 0.8 fusion.12
  89.1 1.7 collective-permute-start.22
  90.8 2.6 %collective-permute-start.21 = (bf16[256,256]{1,0:T(8,128)(2,1)S(1)}, bf16[256,256]{1,0:T(8,128)(2,1)S(1)}, u32[]{:S(2)}, u32[]{:S(2)}) collective-permute-start(bf16[256,256]{1,0:T(8,128)(2,1)S(1)} %get-tuple-element.122), channel_id=1, source_target_pairs={{0,2},{1,3},{2,0},{3,1},{4,6},{5,7},{6,4},{7,5},{8,10},{9,11},{10,... | collective-permute-start | bytes 393224 | tf_op jit(solution)/shard_map/ppermute | solution.py:76
  93.5 1.1 collective-permute-start.20
  95.0 4.3 %collective-permute-done.21 = bf16[256,256]{1,0:T(8,128)(2,1)S(1)} collective-permute-done((bf16[256,256]{1,0:T(8,128)(2,1)S(1)}, bf16[256,256]{1,0:T(8,128)(2,1)S(1)}, u32[]{:S(2)}, u32[]{:S(2)}) %collective-permute-start.21) | collective-permute-done | bytes 131104 | tf_op jit(solution)/shard_map/ppermute | solution.py:76
  100.1 1.4 collective-permute-start.23
  102.2 0.8 collective-permute-done.23
  103.1 0.8 fusion.4.weight_sums
  105.1 4.3 %shard_map.120 = (bf16[1104,256]{1,0:T(8,128)(2,1)}, bf16[1104,256]{1,0:T(8,128)(2,1)}, bf16[1104,256]{1,0:T(8,128)(2,1)}) custom-call(s32[8,256]{1,0:T(8,128)} %shard_map.114.lists, bf16[128,128,128]{2,1,0:T(8,128)(2,1)} %own.11, bf16[128,128,128]{2,1,0:T(8,128)(2,1)} %collective-permute-done.3.sib, bf16[2,128,256]{2,1,0:T(8,128)(2,1)} %bitcast.83, ...), custom_call_target="tpu_custom_call" | custom-call | flops 402653184 | bytes 3145728 | tf_op jit(solution)/shard_map/pallas_call | solution.py:367
  109.4 3.0 %collective-permute-start.25 = (bf16[1104,256]{1,0:T(8,128)(2,1)}, bf16[1104,256]{1,0:T(8,128)(2,1)S(1)}, u32[]{:S(2)}, u32[]{:S(2)}) collective-permute-start(bf16[1104,256]{1,0:T(8,128)(2,1)} %get-tuple-element.95), channel_id=1, source_target_pairs={{4,36},{12,44},{20,52},{28,60},{36,68},{44,76},{52,84},{60,92},{68... | collective-permute-start | bytes 1695752 | tf_op jit(solution)/shard_map/ppermute | solution.py:64
  112.4 9.9 %shard_map.119 = (bf16[1104,256]{1,0:T(8,128)(2,1)}, bf16[1104,256]{1,0:T(8,128)(2,1)}, bf16[1104,256]{1,0:T(8,128)(2,1)}, bf16[1104,256]{1,0:T(8,128)(2,1)}, bf...) custom-call(s32[8,256]{1,0:T(8,128)} %shard_map.114.lists, ...), custom_call_target="tpu_custom_call" | custom-call | flops 1073741824 | bytes 8388608 | tf_op jit(solution)/shard_map/pallas_call | solution.py:367
  122.4 1.2 broadcast_select_fusion
  124.0 1.5 collective-permute-start.26
  125.5 7.0 %collective-permute-done.27.ja2 = bf16[1104,256]{1,0:T(8,128)(2,1)S(1)} collective-permute-done((bf16[1104,256]{1,0:T(8,128)(2,1)S(1)}, bf16[1104,256]{1,0:T(8,128)(2,1)S(1)}, u32[]{:S(2)}, u32[]{:S(2)}) %collective-permute-start.27) | collective-permute-done | bytes 565280 | tf_op jit(solution)/shard_map/ppermute | solution.py:64
  132.5 2.5 %collective-permute-done.26.ja1 = bf16[1104,256]{1,0:T(8,128)(2,1)S(1)} collective-permute-done((bf16[1104,256]{1,0:T(8,128)(2,1)S(1)}, bf16[1104,256]{1,0:T(8,128)(2,1)S(1)}, u32[]{:S(2)}, u32[]{:S(2)}) %collective-permute-start.26) | collective-permute-done | bytes 565280 | tf_op jit(solution)/shard_map/ppermute | solution.py:64
  135.2 1.5 collective-permute-start.29
  137.0 7.0 %collective-permute-done.29 = bf16[1104,256]{1,0:T(8,128)(2,1)S(1)} collective-permute-done((bf16[1104,256]{1,0:T(8,128)(2,1)S(1)}, bf16[1104,256]{1,0:T(8,128)(2,1)S(1)}, u32[]{:S(2)}, u32[]{:S(2)}) %collective-permute-start.29) | collective-permute-done | bytes 565280 | tf_op jit(solution)/shard_map/ppermute | solution.py:64
  144.0 2.9 %collective-permute-done.28.jb1 = bf16[1104,256]{1,0:T(8,128)(2,1)S(1)} collective-permute-done((bf16[1104,256]{1,0:T(8,128)(2,1)S(1)}, bf16[1104,256]{1,0:T(8,128)(2,1)S(1)}, u32[]{:S(2)}, u32[]{:S(2)}) %collective-permute-start.28) | collective-permute-done | bytes 565280 | tf_op jit(solution)/shard_map/ppermute | solution.py:64
  147.5 2.7 %collective-permute-start.31 = (bf16[1104,256]{1,0:T(8,128)(2,1)S(1)}, bf16[1104,256]{1,0:T(8,128)(2,1)S(1)}, u32[]{:S(2)}, u32[]{:S(2)}) collective-permute-start(bf16[1104,256]{1,0:T(8,128)(2,1)S(1)} %add_convert_fusion), channel_id=1, source_target_pairs={{0,24},{4,228},{8,0},{12,236},{16,8},{20,244},{24,16},{28,252},{32... | collective-permute-start | bytes 1695752 | tf_op jit(solution)/shard_map/ppermute | solution.py:64
  150.2 1.0 shard_map.121
  151.2 0.7 collective-permute-start.32
  152.6 4.7 %collective-permute-done.30.jc1 = bf16[1104,256]{1,0:T(8,128)(2,1)S(1)} collective-permute-done((bf16[1104,256]{1,0:T(8,128)(2,1)S(1)}, bf16[1104,256]{1,0:T(8,128)(2,1)S(1)}, u32[]{:S(2)}, u32[]{:S(2)}) %collective-permute-start.30) | collective-permute-done | bytes 565280 | tf_op jit(solution)/shard_map/ppermute | solution.py:64
  157.6 3.9 %collective-permute-start.34 = (bf16[288,256]{1,0:T(8,128)(2,1)S(1)}, bf16[288,256]{1,0:T(8,128)(2,1)S(1)}, u32[]{:S(2)}, u32[]{:S(2)}) collective-permute-start(bf16[288,256]{1,0:T(8,128)(2,1)S(1)} %get-tuple-element.115), channel_id=1, source_target_pairs={{0,32},{4,12},{8,40},{12,20},{16,48},{20,28},{24,56},{28,4},{32,64... | collective-permute-start | bytes 442376 | tf_op jit(solution)/shard_map/ppermute | solution.py:64
  161.4 5.7 %collective-permute-start.35 = (bf16[288,256]{1,0:T(8,128)(2,1)S(1)}, bf16[288,256]{1,0:T(8,128)(2,1)S(1)}, u32[]{:S(2)}, u32[]{:S(2)}) collective-permute-start(bf16[288,256]{1,0:T(8,128)(2,1)S(1)} %get-tuple-element.116), channel_id=1, source_target_pairs={{0,224},{4,28},{8,232},{12,4},{16,240},{20,12},{24,248},{28,20},{3... | collective-permute-start | bytes 442376 | tf_op jit(solution)/shard_map/ppermute | solution.py:64
  167.1 1.1 collective-permute-start.36
  168.2 1.3 collective-permute-done.34.r1
  169.5 3.1 %collective-permute-done.36.r3 = bf16[288,256]{1,0:T(8,128)(2,1)S(1)} collective-permute-done((bf16[288,256]{1,0:T(8,128)(2,1)S(1)}, bf16[288,256]{1,0:T(8,128)(2,1)S(1)}, u32[]{:S(2)}, u32[]{:S(2)}) %collective-permute-start.36) | collective-permute-done | bytes 147488 | tf_op jit(solution)/shard_map/ppermute | solution.py:64
  172.6 0.7 shard_map.124
  173.3 1.3 collective-permute-start.37
  174.6 0.7 shard_map.123
  175.3 7.1 %collective-permute-done.37 = f32[1,256]{1,0:T(1,128)S(1)} collective-permute-done((f32[1,256]{1,0:T(1,128)S(1)}, f32[1,256]{1,0:T(1,128)S(1)}, u32[]{:S(2)}, u32[]{:S(2)}) %collective-permute-start.37) | collective-permute-done | bytes 1056 | tf_op jit(solution)/shard_map/ppermute | solution.py:536
  (139 shorter events, 10.7 us)
Async XLA Ops:
  0.6 13.5 %collective-permute-start.3 = (bf16[128,128,128]{2,1,0:T(8,128)(2,1)}, bf16[128,128,128]{2,1,0:T(8,128)(2,1)}, u32[]{:S(2)}, u32[]{:S(2)}) collective-permute-start(bf16[128,128,128]{2,1,0:T(8,128)(2,1)} %own.11), channel_id=1, source_target_pairs={{0,4},{4,0},{8,12},{12,8},{16,20},{20,16},{24,28},{28,24},{32,36},... | collective-permute-start | bytes 12582920 | tf_op jit(solution)/shard_map/ppermute | solution.py:72
  4.9 9.1 %collective-permute-start.1 = (bf16[272,256]{1,0:T(8,128)(2,1)S(1)}, bf16[272,256]{1,0:T(8,128)(2,1)S(1)}, u32[]{:S(2)}, u32[]{:S(2)}) collective-permute-start(bf16[272,256]{1,0:T(8,128)(2,1)S(1)} %get-tuple-element.136), channel_id=1, source_target_pairs={{0,224},{4,28},{8,232},{12,4},{16,240},{20,12},{24,248},{28,20},{3... | collective-permute-start | bytes 417800 | tf_op jit(solution)/shard_map/ppermute | solution.py:64
  5.7 8.3 %collective-permute-start = (bf16[272,256]{1,0:T(8,128)(2,1)S(1)}, bf16[272,256]{1,0:T(8,128)(2,1)S(1)}, u32[]{:S(2)}, u32[]{:S(2)}) collective-permute-start(bf16[272,256]{1,0:T(8,128)(2,1)S(1)} %get-tuple-element.136), channel_id=1, source_target_pairs={{0,32},{4,12},{8,40},{12,20},{16,48},{20,28},{24,56},{28,4},{32,64... | collective-permute-start | bytes 417800 | tf_op jit(solution)/shard_map/ppermute | solution.py:64
  6.4 7.6 %collective-permute-start.2 = (bf16[272,256]{1,0:T(8,128)(2,1)S(1)}, bf16[272,256]{1,0:T(8,128)(2,1)S(1)}, u32[]{:S(2)}, u32[]{:S(2)}) collective-permute-start(bf16[272,256]{1,0:T(8,128)(2,1)S(1)} %get-tuple-element.136), channel_id=1, source_target_pairs={{0,64},{4,20},{8,72},{12,28},{16,80},{20,4},{24,88},{28,12},{32,96... | collective-permute-start | bytes 417800 | tf_op jit(solution)/shard_map/ppermute | solution.py:64
  8.9 5.1 %copy-start.27 = (s32[3,128]{1,0:T(4,128)}, s32[3,128]{1,0:T(4,128)S(1)}, u32[]{:S(2)}) copy-start(s32[3,128]{1,0:T(4,128)S(1)} %add_add_fusion.1.own) | copy-start | bytes 4612
  8.9 11.0 %collective-permute-start.8 = (s32[3,128]{1,0:T(4,128)S(1)}, s32[3,128]{1,0:T(4,128)S(1)}, u32[]{:S(2)}, u32[]{:S(2)}) collective-permute-start(s32[3,128]{1,0:T(4,128)S(1)} %add_add_fusion.1.own), channel_id=1, source_target_pairs={{0,4},{4,0},{8,12},{12,8},{16,20},{20,16},{24,28},{28,24},{32,36},... | collective-permute-start | bytes 4616 | tf_op jit(solution)/shard_map/ppermute | solution.py:72
  14.1 5.7 %copy-start.7 = (bf16[4,272,256]{2,1,0:T(8,128)(2,1)}, bf16[4,272,256]{2,1,0:T(8,128)(2,1)S(1)}, u32[]{:S(2)}) copy-start(bf16[4,272,256]{2,1,0:T(8,128)(2,1)S(1)} %pad_maximum_fusion.1.rest_0_) | copy-start | bytes 1671172
  14.1 5.6 %copy-start.29 = (s32[128]{0:T(128)S(1)}, s32[128]{0:T(128)}, u32[]{:S(2)}) copy-start(s32[128]{0:T(128)} %param.12) | copy-start | bytes 1540
  14.2 10.6 %collective-permute-start.5 = (bf16[4,272,256]{2,1,0:T(8,128)(2,1)S(1)}, bf16[4,272,256]{2,1,0:T(8,128)(2,1)S(1)}, u32[]{:S(2)}, u32[]{:S(2)}) collective-permute-start(bf16[4,272,256]{2,1,0:T(8,128)(2,1)S(1)} %pad_maximum_fusion.1.rest_0_), channel_id=1, source_target_pairs={{0,24},{4,228},{8,0},{12,236},{16,8},{20,244},{24,16},{28,252},{32... | collective-permute-start | bytes 1671176 | tf_op jit(solution)/shard_map/ppermute | solution.py:64
  18.3 13.3 %collective-permute-start.4 = (bf16[4,272,256]{2,1,0:T(8,128)(2,1)S(1)}, bf16[4,272,256]{2,1,0:T(8,128)(2,1)S(1)}, u32[]{:S(2)}, u32[]{:S(2)}) collective-permute-start(bf16[4,272,256]{2,1,0:T(8,128)(2,1)S(1)} %pad_maximum_fusion.1.rest_0_), channel_id=1, source_target_pairs={{0,8},{4,36},{8,16},{12,44},{16,24},{20,52},{24,0},{28,60},{32,40}... | collective-permute-start | bytes 1671176 | tf_op jit(solution)/shard_map/ppermute | solution.py:64
  18.3 5.2 %collective-permute-start.6 = (bf16[2,272,256]{2,1,0:T(8,128)(2,1)S(1)}, bf16[2,272,256]{2,1,0:T(8,128)(2,1)S(1)}, u32[]{:S(2)}, u32[]{:S(2)}) collective-permute-start(bf16[2,272,256]{2,1,0:T(8,128)(2,1)S(1)} %pad_maximum_fusion.2), channel_id=1, source_target_pairs={{0,64},{8,72},{16,80},{24,88},{32,96},{40,104},{48,112},{56,120},{... | collective-permute-start | bytes 835592 | tf_op jit(solution)/shard_map/ppermute | solution.py:64
  19.0 4.5 %collective-permute-start.7 = (bf16[2,272,256]{2,1,0:T(8,128)(2,1)S(1)}, bf16[2,272,256]{2,1,0:T(8,128)(2,1)S(1)}, u32[]{:S(2)}, u32[]{:S(2)}) collective-permute-start(bf16[2,272,256]{2,1,0:T(8,128)(2,1)S(1)} %pad_maximum_fusion.3), channel_id=1, source_target_pairs={{0,192},{8,200},{16,208},{24,216},{32,224},{40,232},{48,240},{56,2... | collective-permute-start | bytes 835592 | tf_op jit(solution)/shard_map/ppermute | solution.py:64
  20.0 1.8 copy-start.28
  24.8 6.9 %copy-start.8 = (bf16[4,272,256]{2,1,0:T(8,128)(2,1)}, bf16[4,272,256]{2,1,0:T(8,128)(2,1)S(1)}, u32[]{:S(2)}) copy-start(bf16[4,272,256]{2,1,0:T(8,128)(2,1)S(1)} %collective-permute-done.5.rest_2_) | copy-start | bytes 1671172
  31.6 10.5 %copy-start.6 = (bf16[4,272,256]{2,1,0:T(8,128)(2,1)}, bf16[4,272,256]{2,1,0:T(8,128)(2,1)S(1)}, u32[]{:S(2)}) copy-start(bf16[4,272,256]{2,1,0:T(8,128)(2,1)S(1)} %constant_dynamic-update-slice_fusion.rest_2_) | copy-start | bytes 1671172
  31.7 10.4 %collective-permute-start.10 = (bf16[4,272,256]{2,1,0:T(8,128)(2,1)S(1)}, bf16[4,272,256]{2,1,0:T(8,128)(2,1)S(1)}, u32[]{:S(2)}, u32[]{:S(2)}) collective-permute-start(bf16[4,272,256]{2,1,0:T(8,128)(2,1)S(1)} %broadcast_select_fusion.2), channel_id=1, source_target_pairs={{0,24},{4,228},{8,0},{12,236},{16,8},{20,244},{24,16},{28,252},{32... | collective-permute-start | bytes 1671176 | tf_op jit(solution)/shard_map/ppermute | solution.py:64
  32.4 9.7 %collective-permute-start.9 = (bf16[4,272,256]{2,1,0:T(8,128)(2,1)S(1)}, bf16[4,272,256]{2,1,0:T(8,128)(2,1)S(1)}, u32[]{:S(2)}, u32[]{:S(2)}) collective-permute-start(bf16[4,272,256]{2,1,0:T(8,128)(2,1)S(1)} %collective-permute-done.4.rest_1_), channel_id=1, source_target_pairs={{0,8},{4,36},{8,16},{12,44},{16,24},{20,52},{24,0},{28,60},{32,40}... | collective-permute-start | bytes 1671176 | tf_op jit(solution)/shard_map/ppermute | solution.py:64
  42.1 2.8 %copy-start.20 = (bf16[4,272,256]{2,1,0:T(8,128)(2,1)}, bf16[4,272,256]{2,1,0:T(8,128)(2,1)S(1)}, u32[]{:S(2)}) copy-start(bf16[4,272,256]{2,1,0:T(8,128)(2,1)S(1)} %collective-permute-done.10.rest_1_) | copy-start | bytes 1671172
  42.1 2.8 %copy-start.9 = (bf16[4,272,256]{2,1,0:T(8,128)(2,1)}, bf16[4,272,256]{2,1,0:T(8,128)(2,1)S(1)}, u32[]{:S(2)}) copy-start(bf16[4,272,256]{2,1,0:T(8,128)(2,1)S(1)} %collective-permute-done.9.rest_0_) | copy-start | bytes 1671172
  42.1 10.0 %collective-permute-start.11 = (bf16[4,272,256]{2,1,0:T(8,128)(2,1)S(1)}, bf16[4,272,256]{2,1,0:T(8,128)(2,1)S(1)}, u32[]{:S(2)}, u32[]{:S(2)}) collective-permute-start(bf16[4,272,256]{2,1,0:T(8,128)(2,1)S(1)} %broadcast_select_fusion.1), channel_id=1, source_target_pairs={{0,8},{4,36},{8,16},{12,44},{16,24},{20,52},{24,0},{28,60},{32,40}... | collective-permute-start | bytes 1671176 | tf_op jit(solution)/shard_map/ppermute | solution.py:64
  42.2 9.9 %collective-permute-start.12 = (bf16[4,272,256]{2,1,0:T(8,128)(2,1)S(1)}, bf16[4,272,256]{2,1,0:T(8,128)(2,1)S(1)}, u32[]{:S(2)}, u32[]{:S(2)}) collective-permute-start(bf16[4,272,256]{2,1,0:T(8,128)(2,1)S(1)} %collective-permute-done.10.rest_1_), channel_id=1, source_target_pairs={{0,24},{4,228},{8,0},{12,236},{16,8},{20,244},{24,16},{28,252},{32... | collective-permute-start | bytes 1671176 | tf_op jit(solution)/shard_map/ppermute | solution.py:64
  52.1 6.8 %copy-start.10 = (bf16[4,272,256]{2,1,0:T(8,128)(2,1)}, bf16[4,272,256]{2,1,0:T(8,128)(2,1)S(1)}, u32[]{:S(2)}) copy-start(bf16[4,272,256]{2,1,0:T(8,128)(2,1)S(1)} %collective-permute-done.11.rest_0_) | copy-start | bytes 1671172
  52.1 6.8 %copy-start.11 = (bf16[4,272,256]{2,1,0:T(8,128)(2,1)}, bf16[4,272,256]{2,1,0:T(8,128)(2,1)S(1)}, u32[]{:S(2)}) copy-start(bf16[4,272,256]{2,1,0:T(8,128)(2,1)S(1)} %collective-permute-done.12.rest_1_) | copy-start | bytes 1671172
  52.2 12.6 %collective-permute-start.13 = (bf16[2,272,256]{2,1,0:T(8,128)(2,1)S(1)}, bf16[2,272,256]{2,1,0:T(8,128)(2,1)S(1)}, u32[]{:S(2)}, u32[]{:S(2)}) collective-permute-start(bf16[2,272,256]{2,1,0:T(8,128)(2,1)S(1)} %slice.60), channel_id=1, source_target_pairs={{4,36},{12,44},{20,52},{28,60},{36,68},{44,76},{52,84},{60,92},{68... | collective-permute-start | bytes 835592 | tf_op jit(solution)/shard_map/ppermute | solution.py:64
  54.3 10.5 %collective-permute-start.14 = (bf16[2,272,256]{2,1,0:T(8,128)(2,1)S(1)}, bf16[2,272,256]{2,1,0:T(8,128)(2,1)S(1)}, u32[]{:S(2)}, u32[]{:S(2)}) collective-permute-start(bf16[2,272,256]{2,1,0:T(8,128)(2,1)S(1)} %slice.61), channel_id=1, source_target_pairs={{4,228},{12,236},{20,244},{28,252},{36,4},{44,12},{52,20},{60,28},... | collective-permute-start | bytes 835592 | tf_op jit(solution)/shard_map/ppermute | solution.py:64
  69.9 5.9 %collective-permute-start.16 = (bf16[4,8,16,256]{3,2,1,0:T(8,128)(2,1)}, bf16[4,8,16,256]{3,2,1,0:T(8,128)(2,1)S(1)}, u32[]{:S(2)}, u32[]{:S(2)}) collective-permute-start(bf16[4,8,16,256]{3,2,1,0:T(8,128)(2,1)} %get-tuple-element.91), channel_id=1, source_target_pairs={{0,4},{4,0},{8,12},{12,8},{16,20},{20,16},{24,28},{28,24},{32,36},... | collective-permute-start | bytes 786440 | tf_op jit(solution)/shard_map/ppermute | solution.py:72
  74.4 2.5 %collective-permute-start.15 = (f32[2,128,256]{2,1,0:T(8,128)}, f32[2,128,256]{2,1,0:T(8,128)S(1)}, u32[]{:S(2)}, u32[]{:S(2)}) collective-permute-start(f32[2,128,256]{2,1,0:T(8,128)} %get-tuple-element.89), channel_id=1, source_target_pairs={{0,4},{4,0},{8,12},{12,8},{16,20},{20,16},{24,28},{28,24},{32,36},... | collective-permute-start | bytes 786440 | tf_op jit(solution)/shard_map/ppermute | solution.py:72
  76.8 1.0 copy-start.22
  77.8 10.3 %copy-start.26 = (bf16[256,256]{1,0:T(8,128)(2,1)S(1)}, bf16[256,256]{1,0:T(8,128)(2,1)}, u32[]{:S(2)}) copy-start(bf16[256,256]{1,0:T(8,128)(2,1)} %param.15) | copy-start | bytes 393220
  77.8 10.3 %copy-start.30 = (f32[256]{0:T(256)S(1)}, f32[256]{0:T(256)}, u32[]{:S(2)}) copy-start(f32[256]{0:T(256)} %param.10) | copy-start | bytes 3076
  78.6 6.3 %collective-permute-start.18 = (bf16[256,256]{1,0:T(8,128)(2,1)S(1)}, bf16[256,256]{1,0:T(8,128)(2,1)S(1)}, u32[]{:S(2)}, u32[]{:S(2)}) collective-permute-start(bf16[256,256]{1,0:T(8,128)(2,1)S(1)} %convolution_convert_fusion.1), channel_id=1, source_target_pairs={{0,2},{1,3},{2,0},{3,1},{4,6},{5,7},{6,4},{7,5},{8,10},{9,11},{10,... | collective-permute-start | bytes 393224 | tf_op jit(solution)/shard_map/ppermute | solution.py:76
  81.6 6.5 %collective-permute-start.19 = (bf16[256,256]{1,0:T(8,128)(2,1)S(1)}, bf16[256,256]{1,0:T(8,128)(2,1)S(1)}, u32[]{:S(2)}, u32[]{:S(2)}) collective-permute-start(bf16[256,256]{1,0:T(8,128)(2,1)S(1)} %convolution_convert_fusion), channel_id=1, source_target_pairs={{0,3},{1,0},{2,1},{3,2},{4,7},{5,4},{6,5},{7,6},{8,11},{9,8},{10,9... | collective-permute-start | bytes 393224 | tf_op jit(solution)/shard_map/ppermute | solution.py:76
  82.4 5.7 %collective-permute-start.17 = (bf16[256,256]{1,0:T(8,128)(2,1)S(1)}, bf16[256,256]{1,0:T(8,128)(2,1)S(1)}, u32[]{:S(2)}, u32[]{:S(2)}) collective-permute-start(bf16[256,256]{1,0:T(8,128)(2,1)S(1)} %convolution_convert_fusion.2), channel_id=1, source_target_pairs={{0,1},{1,2},{2,3},{3,0},{4,5},{5,6},{6,7},{7,4},{8,9},{9,10},{10,1... | collective-permute-start | bytes 393224 | tf_op jit(solution)/shard_map/ppermute | solution.py:76
  89.1 5.7 %collective-permute-start.22 = (bf16[256,256]{1,0:T(8,128)(2,1)S(1)}, bf16[256,256]{1,0:T(8,128)(2,1)S(1)}, u32[]{:S(2)}, u32[]{:S(2)}) collective-permute-start(bf16[256,256]{1,0:T(8,128)(2,1)S(1)} %get-tuple-element.122), channel_id=1, source_target_pairs={{0,1},{1,2},{2,3},{3,0},{4,5},{5,6},{6,7},{7,4},{8,9},{9,10},{10,1... | collective-permute-start | bytes 393224 | tf_op jit(solution)/shard_map/ppermute | solution.py:76
  90.8 8.5 %collective-permute-start.21 = (bf16[256,256]{1,0:T(8,128)(2,1)S(1)}, bf16[256,256]{1,0:T(8,128)(2,1)S(1)}, u32[]{:S(2)}, u32[]{:S(2)}) collective-permute-start(bf16[256,256]{1,0:T(8,128)(2,1)S(1)} %get-tuple-element.122), channel_id=1, source_target_pairs={{0,2},{1,3},{2,0},{3,1},{4,6},{5,7},{6,4},{7,5},{8,10},{9,11},{10,... | collective-permute-start | bytes 393224 | tf_op jit(solution)/shard_map/ppermute | solution.py:76
  93.5 6.1 %collective-permute-start.20 = (bf16[256,256]{1,0:T(8,128)(2,1)S(1)}, bf16[256,256]{1,0:T(8,128)(2,1)S(1)}, u32[]{:S(2)}, u32[]{:S(2)}) collective-permute-start(bf16[256,256]{1,0:T(8,128)(2,1)S(1)} %get-tuple-element.122), channel_id=1, source_target_pairs={{0,3},{1,0},{2,1},{3,2},{4,7},{5,4},{6,5},{7,6},{8,11},{9,8},{10,9... | collective-permute-start | bytes 393224 | tf_op jit(solution)/shard_map/ppermute | solution.py:76
  100.1 3.0 %collective-permute-start.23 = (f32[520,256]{1,0:T(8,128)S(1)}, f32[520,256]{1,0:T(8,128)S(1)}, u32[]{:S(2)}, u32[]{:S(2)}) collective-permute-start(f32[520,256]{1,0:T(8,128)S(1)} %select_maximum_fusion), channel_id=1, source_target_pairs={{0,4},{4,0},{8,12},{12,8},{16,20},{20,16},{24,28},{28,24},{32,36},... | collective-permute-start | bytes 1597448 | tf_op jit(solution)/shard_map/ppermute | solution.py:72
  102.1 1.9 %copy-start = (bf16[256,256]{1,0:T(8,128)(2,1)}, bf16[256,256]{1,0:T(8,128)(2,1)S(1)}, u32[]{:S(2)}) copy-start(bf16[256,256]{1,0:T(8,128)(2,1)S(1)} %fusion.2.scaled) | copy-start | bytes 393220
  102.1 2.4 %collective-permute-start.24 = (bf16[256,256]{1,0:T(8,128)(2,1)S(1)}, bf16[256,256]{1,0:T(8,128)(2,1)S(1)}, u32[]{:S(2)}, u32[]{:S(2)}) collective-permute-start(bf16[256,256]{1,0:T(8,128)(2,1)S(1)} %fusion.2.scaled), channel_id=1, source_target_pairs={{0,4},{4,0},{8,12},{12,8},{16,20},{20,16},{24,28},{28,24},{32,36},... | collective-permute-start | bytes 393224 | tf_op jit(solution)/shard_map/ppermute | solution.py:72
  109.4 13.0 %copy-start.18 = (bf16[1104,256]{1,0:T(8,128)(2,1)S(1)}, bf16[1104,256]{1,0:T(8,128)(2,1)}, u32[]{:S(2)}) copy-start(bf16[1104,256]{1,0:T(8,128)(2,1)} %get-tuple-element.96) | copy-start | bytes 1695748
  109.4 14.3 %collective-permute-start.25 = (bf16[1104,256]{1,0:T(8,128)(2,1)}, bf16[1104,256]{1,0:T(8,128)(2,1)S(1)}, u32[]{:S(2)}, u32[]{:S(2)}) collective-permute-start(bf16[1104,256]{1,0:T(8,128)(2,1)} %get-tuple-element.95), channel_id=1, source_target_pairs={{4,36},{12,44},{20,52},{28,60},{36,68},{44,76},{52,84},{60,92},{68... | collective-permute-start | bytes 1695752 | tf_op jit(solution)/shard_map/ppermute | solution.py:64
  122.4 1.4 copy-start.16
  122.4 1.4 copy-start.17
  123.6 8.8 %collective-permute-start.27 = (bf16[1104,256]{1,0:T(8,128)(2,1)S(1)}, bf16[1104,256]{1,0:T(8,128)(2,1)S(1)}, u32[]{:S(2)}, u32[]{:S(2)}) collective-permute-start(bf16[1104,256]{1,0:T(8,128)(2,1)S(1)} %broadcast_select_fusion), channel_id=1, source_target_pairs={{0,24},{4,228},{8,0},{12,236},{16,8},{20,244},{24,16},{28,252},{32... | collective-permute-start | bytes 1695752 | tf_op jit(solution)/shard_map/ppermute | solution.py:64
  123.7 11.2 %copy-start.15 = (bf16[1104,256]{1,0:T(8,128)(2,1)S(1)}, bf16[1104,256]{1,0:T(8,128)(2,1)}, u32[]{:S(2)}) copy-start(bf16[1104,256]{1,0:T(8,128)(2,1)} %get-tuple-element.101) | copy-start | bytes 1695748
  124.0 12.8 %copy-start.14 = (bf16[1104,256]{1,0:T(8,128)(2,1)S(1)}, bf16[1104,256]{1,0:T(8,128)(2,1)}, u32[]{:S(2)}) copy-start(bf16[1104,256]{1,0:T(8,128)(2,1)} %get-tuple-element.100) | copy-start | bytes 1695748
  124.0 11.0 %collective-permute-start.26 = (bf16[1104,256]{1,0:T(8,128)(2,1)S(1)}, bf16[1104,256]{1,0:T(8,128)(2,1)S(1)}, u32[]{:S(2)}, u32[]{:S(2)}) collective-permute-start(bf16[1104,256]{1,0:T(8,128)(2,1)S(1)} %fusion.3), channel_id=1, source_target_pairs={{0,8},{4,36},{8,16},{12,44},{16,24},{20,52},{24,0},{28,60},{32,40}... | collective-permute-start | bytes 1695752 | tf_op jit(solution)/shard_map/ppermute | solution.py:64
  135.2 11.8 %copy-start.13 = (bf16[1104,256]{1,0:T(8,128)(2,1)S(1)}, bf16[1104,256]{1,0:T(8,128)(2,1)}, u32[]{:S(2)}) copy-start(bf16[1104,256]{1,0:T(8,128)(2,1)} %get-tuple-element.105) | copy-start | bytes 1695748
  135.2 8.8 %collective-permute-start.29 = (bf16[1104,256]{1,0:T(8,128)(2,1)S(1)}, bf16[1104,256]{1,0:T(8,128)(2,1)S(1)}, u32[]{:S(2)}, u32[]{:S(2)}) collective-permute-start(bf16[1104,256]{1,0:T(8,128)(2,1)S(1)} %add_convert_fusion.2), channel_id=1, source_target_pairs={{0,24},{4,228},{8,0},{12,236},{16,8},{20,244},{24,16},{28,252},{32... | collective-permute-start | bytes 1695752 | tf_op jit(solution)/shard_map/ppermute | solution.py:64
  136.9 10.4 %copy-start.12 = (bf16[1104,256]{1,0:T(8,128)(2,1)S(1)}, bf16[1104,256]{1,0:T(8,128)(2,1)}, u32[]{:S(2)}) copy-start(bf16[1104,256]{1,0:T(8,128)(2,1)} %get-tuple-element.106) | copy-start | bytes 1695748
  136.9 10.1 %collective-permute-start.28 = (bf16[1104,256]{1,0:T(8,128)(2,1)S(1)}, bf16[1104,256]{1,0:T(8,128)(2,1)S(1)}, u32[]{:S(2)}, u32[]{:S(2)}) collective-permute-start(bf16[1104,256]{1,0:T(8,128)(2,1)S(1)} %add_convert_fusion.3), channel_id=1, source_target_pairs={{0,8},{4,36},{8,16},{12,44},{16,24},{20,52},{24,0},{28,60},{32,40}... | collective-permute-start | bytes 1695752 | tf_op jit(solution)/shard_map/ppermute | solution.py:64
  147.2 3.1 %copy-start.2 = (s32[8,256]{1,0:T(8,128)S(1)}, s32[8,256]{1,0:T(8,128)}, u32[]{:S(2)}) copy-start(s32[8,256]{1,0:T(8,128)} %shard_map.114.lists) | copy-start | bytes 24580
  147.2 3.0 %copy-start.4 = (bf16[1104,256]{1,0:T(8,128)(2,1)S(1)}, bf16[1104,256]{1,0:T(8,128)(2,1)}, u32[]{:S(2)}) copy-start(bf16[1104,256]{1,0:T(8,128)(2,1)} %get-tuple-element.92.h0) | copy-start | bytes 1695748
  147.2 3.0 %copy-start.5 = (f32[1,256]{1,0:T(1,128)S(1)}, f32[1,256]{1,0:T(1,128)}, u32[]{:S(2)}) copy-start(f32[1,256]{1,0:T(1,128)} %slice_add_fusion.chip_bias) | copy-start | bytes 3076
  147.2 10.1 %collective-permute-start.30 = (bf16[1104,256]{1,0:T(8,128)(2,1)S(1)}, bf16[1104,256]{1,0:T(8,128)(2,1)S(1)}, u32[]{:S(2)}, u32[]{:S(2)}) collective-permute-start(bf16[1104,256]{1,0:T(8,128)(2,1)S(1)} %add_convert_fusion.1), channel_id=1, source_target_pairs={{0,8},{4,36},{8,16},{12,44},{16,24},{20,52},{24,0},{28,60},{32,40}... | collective-permute-start | bytes 1695752 | tf_op jit(solution)/shard_map/ppermute | solution.py:64
  147.5 9.8 %collective-permute-start.31 = (bf16[1104,256]{1,0:T(8,128)(2,1)S(1)}, bf16[1104,256]{1,0:T(8,128)(2,1)S(1)}, u32[]{:S(2)}, u32[]{:S(2)}) collective-permute-start(bf16[1104,256]{1,0:T(8,128)(2,1)S(1)} %add_convert_fusion), channel_id=1, source_target_pairs={{0,24},{4,228},{8,0},{12,236},{16,8},{20,244},{24,16},{28,252},{32... | collective-permute-start | bytes 1695752 | tf_op jit(solution)/shard_map/ppermute | solution.py:64
  150.2 7.0 %copy-start.3 = (bf16[1104,256]{1,0:T(8,128)(2,1)S(1)}, bf16[1104,256]{1,0:T(8,128)(2,1)}, u32[]{:S(2)}) copy-start(bf16[1104,256]{1,0:T(8,128)(2,1)} %get-tuple-element.104.h1) | copy-start | bytes 1695748
  151.2 1.4 collective-permute-start.32
  151.9 0.7 collective-permute-start.33
  157.2 17.3 %copy-start.1 = (bf16[256,256]{1,0:T(8,128)(2,1)S(1)}, bf16[256,256]{1,0:T(8,128)(2,1)}, u32[]{:S(2)}) copy-start(bf16[256,256]{1,0:T(8,128)(2,1)} %copy-done) | copy-start | bytes 393220
  157.6 12.0 %collective-permute-start.34 = (bf16[288,256]{1,0:T(8,128)(2,1)S(1)}, bf16[288,256]{1,0:T(8,128)(2,1)S(1)}, u32[]{:S(2)}, u32[]{:S(2)}) collective-permute-start(bf16[288,256]{1,0:T(8,128)(2,1)S(1)} %get-tuple-element.115), channel_id=1, source_target_pairs={{0,32},{4,12},{8,40},{12,20},{16,48},{20,28},{24,56},{28,4},{32,64... | collective-permute-start | bytes 442376 | tf_op jit(solution)/shard_map/ppermute | solution.py:64
  161.4 8.1 %collective-permute-start.35 = (bf16[288,256]{1,0:T(8,128)(2,1)S(1)}, bf16[288,256]{1,0:T(8,128)(2,1)S(1)}, u32[]{:S(2)}, u32[]{:S(2)}) collective-permute-start(bf16[288,256]{1,0:T(8,128)(2,1)S(1)} %get-tuple-element.116), channel_id=1, source_target_pairs={{0,224},{4,28},{8,232},{12,4},{16,240},{20,12},{24,248},{28,20},{3... | collective-permute-start | bytes 442376 | tf_op jit(solution)/shard_map/ppermute | solution.py:64
  167.1 5.5 %collective-permute-start.36 = (bf16[288,256]{1,0:T(8,128)(2,1)S(1)}, bf16[288,256]{1,0:T(8,128)(2,1)S(1)}, u32[]{:S(2)}, u32[]{:S(2)}) collective-permute-start(bf16[288,256]{1,0:T(8,128)(2,1)S(1)} %get-tuple-element.117), channel_id=1, source_target_pairs={{0,64},{4,20},{8,72},{12,28},{16,80},{20,4},{24,88},{28,12},{32,96... | collective-permute-start | bytes 442376 | tf_op jit(solution)/shard_map/ppermute | solution.py:64
  173.3 9.1 %collective-permute-start.37 = (f32[1,256]{1,0:T(1,128)S(1)}, f32[1,256]{1,0:T(1,128)S(1)}, u32[]{:S(2)}, u32[]{:S(2)}) collective-permute-start(f32[1,256]{1,0:T(1,128)S(1)} %shard_map.124), channel_id=1, source_target_pairs={{0,4},{8,12},{16,20},{24,28},{32,36},{40,44},{48,52},{56,60},{64,6... | collective-permute-start | bytes 3080 | tf_op jit(solution)/shard_map/ppermute | solution.py:536
  (5 other events, 3.9 us)
where the time goes:
time: 184 us; the launch traced here: 183 us
  starting transfers between devices  61.7 us (34%)
  waiting for transfers between devices  60.9 us (33%)
  Pallas kernels  38.8 us (21%)
  other arithmetic  11.9 us (6%)
  local copies, waits for them, and re-layouts  5.01 us (3%)
  matrix products  2.48 us (1%)
  between operations  2.18 us (1%)
    ppermute x25, waiting for transfers between devices, shift(): return lax.ppermute(value, 'dom', pairs)  42.6 us
    ppermute x25, starting transfers between devices, shift(): return lax.ppermute(value, 'dom', pairs)  39.4 us
    pallas_call x4, Pallas kernels, forward(): pl.pallas_call(functools.partial(forward_kernel, call), out_shape=(jax.Sh...  20.1 us
    pallas_call x2, Pallas kernels, backward(): pl.pallas_call(functools.partial(backward_kernel, call), out_shape=tuple(...  14.2 us
    ppermute x6, starting transfers between devices, swap(): lax.ppermute(value, 'dom', [(i, i ^ bit) for i in range(NZ * NX * 2)])  11.1 us
    ppermute x6, starting transfers between devices, y_shift(): return lax.ppermute(value, 'feat', [(y, (y + dy) % NY) for y in range(NY)])  9.88 us
    ppermute x6, waiting for transfers between devices, y_shift(): return lax.ppermute(value, 'feat', [(y, (y + dy) % NY) for y in range(NY)])  9.11 us
    ppermute x1, waiting for transfers between devices, scatter(): lax.ppermute(bias, 'dom', [(i, i + 1) for i in range(0, NZ * NX * 2, 2)])  7.08 us
  transfers between devices with their start and end apart: 38, of which 17 were waited for; matrix products, arithmetic and copies ran while one was open for 7% of the time, Pallas kernels for 16%

commit v1 on v0

--- a/solution.py
+++ b/solution.py
@@ -374,7 +374,7 @@
             pltpu.VMEM((2 * SLOTS + 1, BLK, BLK), BF16),
             pltpu.SemaphoreType.DMA((2 * SLOTS // FETCH,)),
         ],
-        compiler_params=pltpu.CompilerParams(vmem_limit_bytes=VMEM),
+        compiler_params=pltpu.CompilerParams(vmem_limit_bytes=44 * MIB),
         cost_estimate=pl.CostEstimate(
             flops=2 * BLK * BLK * WIDTH * len(shapes) * 16, bytes_accessed=len(shapes) * MIB, transcendentals=0
         ),

time: 184 us -> 179 us (0.973)
  Pallas kernels: 38.8 us -> 27.1 us
  waiting for transfers between devices: 60.9 us -> 69.6 us
  starting transfers between devices: 61.7 us -> 64.3 us
  other arithmetic: 11.9 us -> 9.55 us
    pallas_call x2, Pallas kernels: 14.2 us -> 5.25 us  [backward(): pl.pallas_call(functools.partial(backward_kernel, call), out_shape=tuple(...]
    ppermute x25, waiting for transfers between devices: 42.6 us -> 48.8 us  [shift(): return lax.ppermute(value, 'dom', pairs)]
    pallas_call x4, Pallas kernels: 20.1 us -> 17.3 us  [forward(): pl.pallas_call(functools.partial(forward_kernel, call), out_shape=(jax.Sh...]
    ppermute x1, waiting for transfers between devices: 7.08 us -> 9.33 us  [scatter(): lax.ppermute(bias, 'dom', [(i, i + 1) for i in range(0, NZ * NX * 2, 2)])]
    ppermute x25, starting transfers between devices: 39.4 us -> 41.4 us  [shift(): return lax.ppermute(value, 'dom', pairs)]
  transfers between devices with their start and end apart: 38 -> 38, of which waited for: 17 -> 19; matrix products, arithmetic and copies ran while one was open for 7% -> 6% of each run, Pallas kernels for 16% -> 11%
where the time goes in v1:
time: 179 us; the launch traced here: 180 us
  waiting for transfers between devices  69.6 us (39%)
  starting transfers between devices  64.3 us (36%)
  Pallas kernels  27.1 us (15%)
  other arithmetic  9.55 us (5%)
  local copies, waits for them, and re-layouts  4.69 us (3%)
  matrix products  2.48 us (1%)
  between operations  2.08 us (1%)
    ppermute x25, waiting for transfers between devices, shift(): return lax.ppermute(value, 'dom', pairs)  48.8 us
    ppermute x25, starting transfers between devices, shift(): return lax.ppermute(value, 'dom', pairs)  41.4 us
    pallas_call x4, Pallas kernels, forward(): pl.pallas_call(functools.partial(forward_kernel, call), out_shape=(jax.Sh...  17.3 us
    ppermute x6, starting transfers between devices, swap(): lax.ppermute(value, 'dom', [(i, i ^ bit) for i in range(NZ * NX * 2)])  11.7 us
    ppermute x6, starting transfers between devices, y_shift(): return lax.ppermute(value, 'feat', [(y, (y + dy) % NY) for y in range(NY)])  9.89 us
    ppermute x1, waiting for transfers between devices, scatter(): lax.ppermute(bias, 'dom', [(i, i + 1) for i in range(0, NZ * NX * 2, 2)])  9.33 us
    ppermute x6, waiting for transfers between devices, y_shift(): return lax.ppermute(value, 'feat', [(y, (y + dy) % NY) for y in range(NY)])  9.11 us
    pallas_call x2, Pallas kernels, backward(): pl.pallas_call(functools.partial(backward_kernel, call), out_shape=tuple(...  5.25 us
  transfers between devices with their start and end apart: 38, of which 19 were waited for; matrix products, arithmetic and copies ran while one was open for 6% of the time, Pallas kernels for 11%

profile of v1, /device:TPU:1, one launch (start us, length us, event | category | flops | bytes accessed | tf_op | source)
XLA Modules:
  0.0 179.8 jit_solution(17235230597119796593)
XLA Ops:
  0.6 3.3 %collective-permute-start.3 = (bf16[128,128,128]{2,1,0:T(8,128)(2,1)}, bf16[128,128,128]{2,1,0:T(8,128)(2,1)}, u32[]{:S(2)}, u32[]{:S(2)}) collective-permute-start(bf16[128,128,128]{2,1,0:T(8,128)(2,1)} %own.11), channel_id=1, source_target_pairs={{0,4},{4,0},{8,12},{12,8},{16,20},{20,16},{24,28},{28,24},{32,36},... | collective-permute-start | bytes 12582920 | tf_op jit(solution)/shard_map/ppermute | solution.py:72
  4.0 0.9 fusion.11
  4.9 0.8 collective-permute-start.1
  5.7 0.7 collective-permute-start
  6.4 1.0 collective-permute-start.2
  8.2 0.7 add_add_fusion.1.own
  8.9 1.7 collective-permute-start.8
  10.6 3.4 %convert_reduce_fusion = f32[128,128]{1,0:T(8,128)S(1)} fusion(bf16[128,128,128]{2,1,0:T(8,128)(2,1)} %own.11), kind=kLoop, calls=%fused_computation | loop fusion | flops 4177920 | bytes 4259840 | tf_op jit(solution)/shard_map/reduce_sum | solution.py:561
  14.2 4.1 %collective-permute-start.5 = (bf16[4,272,256]{2,1,0:T(8,128)(2,1)S(1)}, bf16[4,272,256]{2,1,0:T(8,128)(2,1)S(1)}, u32[]{:S(2)}, u32[]{:S(2)}) collective-permute-start(bf16[4,272,256]{2,1,0:T(8,128)(2,1)S(1)} %pad_maximum_fusion.1.rest_0_), channel_id=1, source_target_pairs={{0,24},{4,228},{8,0},{12,236},{16,8},{20,244},{24,16},{28,252},{32... | collective-permute-start | bytes 1671176 | tf_op jit(solution)/shard_map/ppermute | solution.py:64
  20.5 1.2 stack.83.place
  21.7 1.8 %shard_map.114.lists = s32[8,256]{1,0:T(8,128)} custom-call(s32[6]{0:T(128)} %stack.83.place, s32[3,128]{1,0:T(4,128)} %copy-done.15, s32[3,128]{1,0:T(4,128)} %copy-done.16), custom_call_target="tpu_custom_call" | custom-call | tf_op jit(solution)/shard_map/pallas_call | solution.py:141
  23.5 1.2 collective-permute-done.5.rest_2_
  24.8 6.8 %collective-permute-done.4.rest_1_ = bf16[4,272,256]{2,1,0:T(8,128)(2,1)S(1)} collective-permute-done((bf16[4,272,256]{2,1,0:T(8,128)(2,1)S(1)}, bf16[4,272,256]{2,1,0:T(8,128)(2,1)S(1)}, u32[]{:S(2)}, u32[]{:S(2)}) %collective-permute-start.4) | collective-permute-done | bytes 557088 | tf_op jit(solution)/shard_map/ppermute | solution.py:64
  32.4 0.9 collective-permute-start.9
  33.2 4.3 %shard_map.115 = (f32[2,128,256]{2,1,0:T(8,128)}, f32[2,128,256]{2,1,0:T(8,128)}, bf16[4,8,16,256]{3,2,1,0:T(8,128)(2,1)}) custom-call(s32[8,256]{1,0:T(8,128)} %shard_map.114.lists, bf16[128,128,128]{2,1,0:T(8,128)(2,1)} %own.11, bf16[128,128,128]{2,1,0:T(8,128)(2,1)} %collective-permute-done.3.sib, bf16[4,272,256]{2,1,0:T(8,128)(2,1)} %copy-done.3, ...), custom_call_target="tpu_custom_call" | custom-call | flops 402653184 | bytes 3145728 | tf_op jit(solution)/shard_map/pallas_call | solution.py:285
  37.6 4.5 %collective-permute-done.10.rest_1_ = bf16[4,272,256]{2,1,0:T(8,128)(2,1)S(1)} collective-permute-done((bf16[4,272,256]{2,1,0:T(8,128)(2,1)S(1)}, bf16[4,272,256]{2,1,0:T(8,128)(2,1)S(1)}, u32[]{:S(2)}, u32[]{:S(2)}) %collective-permute-start.10) | collective-permute-done | bytes 557088 | tf_op jit(solution)/shard_map/ppermute | solution.py:64
  42.2 2.7 %collective-permute-start.12 = (bf16[4,272,256]{2,1,0:T(8,128)(2,1)S(1)}, bf16[4,272,256]{2,1,0:T(8,128)(2,1)S(1)}, u32[]{:S(2)}, u32[]{:S(2)}) collective-permute-start(bf16[4,272,256]{2,1,0:T(8,128)(2,1)S(1)} %collective-permute-done.10.rest_1_), channel_id=1, source_target_pairs={{0,24},{4,228},{8,0},{12,236},{16,8},{20,244},{24,16},{28,252},{32... | collective-permute-start | bytes 1671176 | tf_op jit(solution)/shard_map/ppermute | solution.py:64
  44.9 4.4 %shard_map.116 = (f32[2,128,256]{2,1,0:T(8,128)}, f32[2,128,256]{2,1,0:T(8,128)}, bf16[4,8,16,256]{3,2,1,0:T(8,128)(2,1)}) custom-call(s32[8,256]{1,0:T(8,128)} %shard_map.114.lists, bf16[128,128,128]{2,1,0:T(8,128)(2,1)} %own.11, bf16[128,128,128]{2,1,0:T(8,128)(2,1)} %collective-permute-done.3.sib, bf16[4,272,256]{2,1,0:T(8,128)(2,1)} %copy-done.5, ...), custom_call_target="tpu_custom_call" | custom-call | flops 402653184 | bytes 3145728 | tf_op jit(solution)/shard_map/pallas_call | solution.py:285
  49.3 2.8 %collective-permute-done.11.rest_0_ = bf16[4,272,256]{2,1,0:T(8,128)(2,1)S(1)} collective-permute-done((bf16[4,272,256]{2,1,0:T(8,128)(2,1)S(1)}, bf16[4,272,256]{2,1,0:T(8,128)(2,1)S(1)}, u32[]{:S(2)}, u32[]{:S(2)}) %collective-permute-start.11) | collective-permute-done | bytes 557088 | tf_op jit(solution)/shard_map/ppermute | solution.py:64
  52.2 2.1 %collective-permute-start.13 = (bf16[2,272,256]{2,1,0:T(8,128)(2,1)S(1)}, bf16[2,272,256]{2,1,0:T(8,128)(2,1)S(1)}, u32[]{:S(2)}, u32[]{:S(2)}) collective-permute-start(bf16[2,272,256]{2,1,0:T(8,128)(2,1)S(1)} %slice.60), channel_id=1, source_target_pairs={{4,36},{12,44},{20,52},{28,60},{36,68},{44,76},{52,84},{60,92},{68... | collective-permute-start | bytes 835592 | tf_op jit(solution)/shard_map/ppermute | solution.py:64
  54.3 4.6 %collective-permute-start.14 = (bf16[2,272,256]{2,1,0:T(8,128)(2,1)S(1)}, bf16[2,272,256]{2,1,0:T(8,128)(2,1)S(1)}, u32[]{:S(2)}, u32[]{:S(2)}) collective-permute-start(bf16[2,272,256]{2,1,0:T(8,128)(2,1)S(1)} %slice.61), channel_id=1, source_target_pairs={{4,228},{12,236},{20,244},{28,252},{36,4},{44,12},{52,20},{60,28},... | collective-permute-start | bytes 835592 | tf_op jit(solution)/shard_map/ppermute | solution.py:64
  58.9 4.4 %shard_map.117 = (f32[2,128,256]{2,1,0:T(8,128)}, f32[2,128,256]{2,1,0:T(8,128)}, bf16[4,8,16,256]{3,2,1,0:T(8,128)(2,1)}) custom-call(s32[8,256]{1,0:T(8,128)} %shard_map.114.lists, bf16[128,128,128]{2,1,0:T(8,128)(2,1)} %own.11, bf16[128,128,128]{2,1,0:T(8,128)(2,1)} %collective-permute-done.3.sib, bf16[4,272,256]{2,1,0:T(8,128)(2,1)} %copy-done.6, ...), custom_call_target="tpu_custom_call" | custom-call | flops 268435456 | bytes 2097152 | tf_op jit(solution)/shard_map/pallas_call | solution.py:285
  63.4 0.7 copy-done.11
  64.1 4.2 %shard_map.118 = (f32[2,128,256]{2,1,0:T(8,128)}, f32[2,128,256]{2,1,0:T(8,128)}, bf16[4,8,16,256]{3,2,1,0:T(8,128)(2,1)}) custom-call(s32[8,256]{1,0:T(8,128)} %shard_map.114.lists, bf16[128,128,128]{2,1,0:T(8,128)(2,1)} %own.11, bf16[128,128,128]{2,1,0:T(8,128)(2,1)} %collective-permute-done.3.sib, bf16[2,272,256]{2,1,0:T(8,128)(2,1)} %copy-done.11, ...), custom_call_target="tpu_custom_call" | custom-call | flops 268435456 | bytes 2097152 | tf_op jit(solution)/shard_map/pallas_call | solution.py:285
  68.3 5.1 %collective-permute-start.16 = (bf16[4,8,16,256]{3,2,1,0:T(8,128)(2,1)}, bf16[4,8,16,256]{3,2,1,0:T(8,128)(2,1)S(1)}, u32[]{:S(2)}, u32[]{:S(2)}) collective-permute-start(bf16[4,8,16,256]{3,2,1,0:T(8,128)(2,1)} %get-tuple-element.91), channel_id=1, source_target_pairs={{0,4},{4,0},{8,12},{12,8},{16,20},{20,16},{24,28},{28,24},{32,36},... | collective-permute-start | bytes 786440 | tf_op jit(solution)/shard_map/ppermute | solution.py:72
  73.5 1.3 collective-permute-done.16
  74.8 1.0 select_bitcast_fusion.1
  76.0 0.8 copy-done.13
  77.7 3.0 %collective-permute-start.18 = (bf16[256,256]{1,0:T(8,128)(2,1)S(1)}, bf16[256,256]{1,0:T(8,128)(2,1)S(1)}, u32[]{:S(2)}, u32[]{:S(2)}) collective-permute-start(bf16[256,256]{1,0:T(8,128)(2,1)S(1)} %convolution_convert_fusion.1), channel_id=1, source_target_pairs={{0,2},{1,3},{2,0},{3,1},{4,6},{5,7},{6,4},{7,5},{8,10},{9,11},{10,... | collective-permute-start | bytes 393224 | tf_op jit(solution)/shard_map/ppermute | solution.py:76
  80.7 0.8 collective-permute-start.19
  81.4 0.7 collective-permute-start.17
  82.3 1.6 collective-permute-done.18
  84.0 3.1 %collective-permute-done.19 = bf16[256,256]{1,0:T(8,128)(2,1)S(1)} collective-permute-done((bf16[256,256]{1,0:T(8,128)(2,1)S(1)}, bf16[256,256]{1,0:T(8,128)(2,1)S(1)}, u32[]{:S(2)}, u32[]{:S(2)}) %collective-permute-start.19) | collective-permute-done | bytes 131104 | tf_op jit(solution)/shard_map/ppermute | solution.py:76
  87.1 0.8 fusion.12
  88.1 1.8 collective-permute-start.22
  89.9 2.6 %collective-permute-start.21 = (bf16[256,256]{1,0:T(8,128)(2,1)S(1)}, bf16[256,256]{1,0:T(8,128)(2,1)S(1)}, u32[]{:S(2)}, u32[]{:S(2)}) collective-permute-start(bf16[256,256]{1,0:T(8,128)(2,1)S(1)} %get-tuple-element.122), channel_id=1, source_target_pairs={{0,2},{1,3},{2,0},{3,1},{4,6},{5,7},{6,4},{7,5},{8,10},{9,11},{10,... | collective-permute-start | bytes 393224 | tf_op jit(solution)/shard_map/ppermute | solution.py:76
  92.5 1.1 collective-permute-start.20
  94.1 4.3 %collective-permute-done.21 = bf16[256,256]{1,0:T(8,128)(2,1)S(1)} collective-permute-done((bf16[256,256]{1,0:T(8,128)(2,1)S(1)}, bf16[256,256]{1,0:T(8,128)(2,1)S(1)}, u32[]{:S(2)}, u32[]{:S(2)}) %collective-permute-start.21) | collective-permute-done | bytes 131104 | tf_op jit(solution)/shard_map/ppermute | solution.py:76
  99.1 1.4 collective-permute-start.23
  101.2 0.9 collective-permute-done.23
  103.0 2.0 %shard_map.120 = (bf16[1104,256]{1,0:T(8,128)(2,1)S(1)}, bf16[1104,256]{1,0:T(8,128)(2,1)S(1)}, bf16[1104,256]{1,0:T(8,128)(2,1)S(1)}) custom-call(s32[8,256]{1,0:T(8,128)S(1)} %copy-done.1, bf16[128,128,128]{2,1,0:T(8,128)(2,1)S(1)} %copy-done, bf16[128,128,128]{2,1,0:T(8,128)(2,1)} %collective-permute-done.3.sib, bf16[2,128,256]{2,1,0:T(8,128)(2,1)S(1)} %bitcast.83, ...), custom_call_target="tpu_custom_call" | custom-call | flops 402653184 | bytes 3145728 | tf_op jit(solution)/shard_map/pallas_call | solution.py:367
  105.0 4.2 %collective-permute-start.25 = (bf16[1104,256]{1,0:T(8,128)(2,1)S(1)}, bf16[1104,256]{1,0:T(8,128)(2,1)S(1)}, u32[]{:S(2)}, u32[]{:S(2)}) collective-permute-start(bf16[1104,256]{1,0:T(8,128)(2,1)S(1)} %get-tuple-element.95), channel_id=1, source_target_pairs={{4,36},{12,44},{20,52},{28,60},{36,68},{44,76},{52,84},{60,92},{68... | collective-permute-start | bytes 1695752 | tf_op jit(solution)/shard_map/ppermute | solution.py:64
  109.2 3.3 %shard_map.119 = (bf16[1104,256]{1,0:T(8,128)(2,1)S(1)}, bf16[1104,256]{1,0:T(8,128)(2,1)S(1)}, bf16[1104,256]{1,0:T(8,128)(2,1)S(1)}, bf16[1104,256]{1,0:T(8,12...) custom-call(s32[8,256]{1,0:T(8,128)S(1)} %copy-done.1, ...), custom_call_target="tpu_custom_call" | custom-call | flops 1073741824 | bytes 8388608 | tf_op jit(solution)/shard_map/pallas_call | solution.py:367
  112.5 4.8 %collective-permute-start.27 = (bf16[1104,256]{1,0:T(8,128)(2,1)S(1)}, bf16[1104,256]{1,0:T(8,128)(2,1)S(1)}, u32[]{:S(2)}, u32[]{:S(2)}) collective-permute-start(bf16[1104,256]{1,0:T(8,128)(2,1)S(1)} %broadcast_select_fusion), channel_id=1, source_target_pairs={{0,24},{4,228},{8,0},{12,236},{16,8},{20,244},{24,16},{28,252},{32... | collective-permute-start | bytes 1695752 | tf_op jit(solution)/shard_map/ppermute | solution.py:64
  117.3 2.9 %collective-permute-done.25 = bf16[1104,256]{1,0:T(8,128)(2,1)S(1)} collective-permute-done((bf16[1104,256]{1,0:T(8,128)(2,1)S(1)}, bf16[1104,256]{1,0:T(8,128)(2,1)S(1)}, u32[]{:S(2)}, u32[]{:S(2)}) %collective-permute-start.25) | collective-permute-done | bytes 565280 | tf_op jit(solution)/shard_map/ppermute | solution.py:64
  120.5 3.3 %collective-permute-done.27.ja2 = bf16[1104,256]{1,0:T(8,128)(2,1)S(1)} collective-permute-done((bf16[1104,256]{1,0:T(8,128)(2,1)S(1)}, bf16[1104,256]{1,0:T(8,128)(2,1)S(1)}, u32[]{:S(2)}, u32[]{:S(2)}) %collective-permute-start.27) | collective-permute-done | bytes 565280 | tf_op jit(solution)/shard_map/ppermute | solution.py:64
  123.8 6.3 %collective-permute-done.26.ja1 = bf16[1104,256]{1,0:T(8,128)(2,1)S(1)} collective-permute-done((bf16[1104,256]{1,0:T(8,128)(2,1)S(1)}, bf16[1104,256]{1,0:T(8,128)(2,1)S(1)}, u32[]{:S(2)}, u32[]{:S(2)}) %collective-permute-start.26) | collective-permute-done | bytes 565280 | tf_op jit(solution)/shard_map/ppermute | solution.py:64
  130.4 0.9 collective-permute-start.29
  131.4 0.7 collective-permute-start.28
  132.2 6.8 %collective-permute-done.29 = bf16[1104,256]{1,0:T(8,128)(2,1)S(1)} collective-permute-done((bf16[1104,256]{1,0:T(8,128)(2,1)S(1)}, bf16[1104,256]{1,0:T(8,128)(2,1)S(1)}, u32[]{:S(2)}, u32[]{:S(2)}) %collective-permute-start.29) | collective-permute-done | bytes 565280 | tf_op jit(solution)/shard_map/ppermute | solution.py:64
  138.9 2.3 %collective-permute-done.28.jb1 = bf16[1104,256]{1,0:T(8,128)(2,1)S(1)} collective-permute-done((bf16[1104,256]{1,0:T(8,128)(2,1)S(1)}, bf16[1104,256]{1,0:T(8,128)(2,1)S(1)}, u32[]{:S(2)}, u32[]{:S(2)}) %collective-permute-start.28) | collective-permute-done | bytes 565280 | tf_op jit(solution)/shard_map/ppermute | solution.py:64
  141.7 2.7 %collective-permute-start.31 = (bf16[1104,256]{1,0:T(8,128)(2,1)S(1)}, bf16[1104,256]{1,0:T(8,128)(2,1)S(1)}, u32[]{:S(2)}, u32[]{:S(2)}) collective-permute-start(bf16[1104,256]{1,0:T(8,128)(2,1)S(1)} %add_convert_fusion), channel_id=1, source_target_pairs={{0,24},{4,228},{8,0},{12,236},{16,8},{20,244},{24,16},{28,252},{32... | collective-permute-start | bytes 1695752 | tf_op jit(solution)/shard_map/ppermute | solution.py:64
  144.4 1.0 shard_map.121
  145.4 0.7 collective-permute-start.32
  146.8 7.4 %collective-permute-done.30.jc1 = bf16[1104,256]{1,0:T(8,128)(2,1)S(1)} collective-permute-done((bf16[1104,256]{1,0:T(8,128)(2,1)S(1)}, bf16[1104,256]{1,0:T(8,128)(2,1)S(1)}, u32[]{:S(2)}, u32[]{:S(2)}) %collective-permute-start.30) | collective-permute-done | bytes 565280 | tf_op jit(solution)/shard_map/ppermute | solution.py:64
  154.5 1.9 %collective-permute-start.34 = (bf16[288,256]{1,0:T(8,128)(2,1)S(1)}, bf16[288,256]{1,0:T(8,128)(2,1)S(1)}, u32[]{:S(2)}, u32[]{:S(2)}) collective-permute-start(bf16[288,256]{1,0:T(8,128)(2,1)S(1)} %get-tuple-element.115), channel_id=1, source_target_pairs={{0,32},{4,12},{8,40},{12,20},{16,48},{20,28},{24,56},{28,4},{32,64... | collective-permute-start | bytes 442376 | tf_op jit(solution)/shard_map/ppermute | solution.py:64
  156.4 5.2 %collective-permute-start.35 = (bf16[288,256]{1,0:T(8,128)(2,1)S(1)}, bf16[288,256]{1,0:T(8,128)(2,1)S(1)}, u32[]{:S(2)}, u32[]{:S(2)}) collective-permute-start(bf16[288,256]{1,0:T(8,128)(2,1)S(1)} %get-tuple-element.116), channel_id=1, source_target_pairs={{0,224},{4,28},{8,232},{12,4},{16,240},{20,12},{24,248},{28,20},{3... | collective-permute-start | bytes 442376 | tf_op jit(solution)/shard_map/ppermute | solution.py:64
  161.6 1.1 collective-permute-start.36
  162.7 1.3 collective-permute-done.34.r1
  164.1 3.1 %collective-permute-done.36.r3 = bf16[288,256]{1,0:T(8,128)(2,1)S(1)} collective-permute-done((bf16[288,256]{1,0:T(8,128)(2,1)S(1)}, bf16[288,256]{1,0:T(8,128)(2,1)S(1)}, u32[]{:S(2)}, u32[]{:S(2)}) %collective-permute-start.36) | collective-permute-done | bytes 147488 | tf_op jit(solution)/shard_map/ppermute | solution.py:64
  167.1 0.7 shard_map.124
  167.8 1.3 collective-permute-start.37
  169.1 0.7 shard_map.123
  169.9 9.3 %collective-permute-done.37 = f32[1,256]{1,0:T(1,128)S(1)} collective-permute-done((f32[1,256]{1,0:T(1,128)S(1)}, f32[1,256]{1,0:T(1,128)S(1)}, u32[]{:S(2)}, u32[]{:S(2)}) %collective-permute-start.37) | collective-permute-done | bytes 1056 | tf_op jit(solution)/shard_map/ppermute | solution.py:536
  (115 shorter events, 10.2 us)
Async XLA Ops:
  0.6 13.5 %collective-permute-start.3 = (bf16[128,128,128]{2,1,0:T(8,128)(2,1)}, bf16[128,128,128]{2,1,0:T(8,128)(2,1)}, u32[]{:S(2)}, u32[]{:S(2)}) collective-permute-start(bf16[128,128,128]{2,1,0:T(8,128)(2,1)} %own.11), channel_id=1, source_target_pairs={{0,4},{4,0},{8,12},{12,8},{16,20},{20,16},{24,28},{28,24},{32,36},... | collective-permute-start | bytes 12582920 | tf_op jit(solution)/shard_map/ppermute | solution.py:72
  4.9 9.1 %collective-permute-start.1 = (bf16[272,256]{1,0:T(8,128)(2,1)S(1)}, bf16[272,256]{1,0:T(8,128)(2,1)S(1)}, u32[]{:S(2)}, u32[]{:S(2)}) collective-permute-start(bf16[272,256]{1,0:T(8,128)(2,1)S(1)} %get-tuple-element.136), channel_id=1, source_target_pairs={{0,224},{4,28},{8,232},{12,4},{16,240},{20,12},{24,248},{28,20},{3... | collective-permute-start | bytes 417800 | tf_op jit(solution)/shard_map/ppermute | solution.py:64
  5.7 8.3 %collective-permute-start = (bf16[272,256]{1,0:T(8,128)(2,1)S(1)}, bf16[272,256]{1,0:T(8,128)(2,1)S(1)}, u32[]{:S(2)}, u32[]{:S(2)}) collective-permute-start(bf16[272,256]{1,0:T(8,128)(2,1)S(1)} %get-tuple-element.136), channel_id=1, source_target_pairs={{0,32},{4,12},{8,40},{12,20},{16,48},{20,28},{24,56},{28,4},{32,64... | collective-permute-start | bytes 417800 | tf_op jit(solution)/shard_map/ppermute | solution.py:64
  6.4 7.6 %collective-permute-start.2 = (bf16[272,256]{1,0:T(8,128)(2,1)S(1)}, bf16[272,256]{1,0:T(8,128)(2,1)S(1)}, u32[]{:S(2)}, u32[]{:S(2)}) collective-permute-start(bf16[272,256]{1,0:T(8,128)(2,1)S(1)} %get-tuple-element.136), channel_id=1, source_target_pairs={{0,64},{4,20},{8,72},{12,28},{16,80},{20,4},{24,88},{28,12},{32,96... | collective-permute-start | bytes 417800 | tf_op jit(solution)/shard_map/ppermute | solution.py:64
  8.9 5.1 %copy-start.15 = (s32[3,128]{1,0:T(4,128)}, s32[3,128]{1,0:T(4,128)S(1)}, u32[]{:S(2)}) copy-start(s32[3,128]{1,0:T(4,128)S(1)} %add_add_fusion.1.own) | copy-start | bytes 4612
  8.9 11.0 %collective-permute-start.8 = (s32[3,128]{1,0:T(4,128)S(1)}, s32[3,128]{1,0:T(4,128)S(1)}, u32[]{:S(2)}, u32[]{:S(2)}) collective-permute-start(s32[3,128]{1,0:T(4,128)S(1)} %add_add_fusion.1.own), channel_id=1, source_target_pairs={{0,4},{4,0},{8,12},{12,8},{16,20},{20,16},{24,28},{28,24},{32,36},... | collective-permute-start | bytes 4616 | tf_op jit(solution)/shard_map/ppermute | solution.py:72
  14.1 5.7 %copy-start.3 = (bf16[4,272,256]{2,1,0:T(8,128)(2,1)}, bf16[4,272,256]{2,1,0:T(8,128)(2,1)S(1)}, u32[]{:S(2)}) copy-start(bf16[4,272,256]{2,1,0:T(8,128)(2,1)S(1)} %pad_maximum_fusion.1.rest_0_) | copy-start | bytes 1671172
  14.1 5.6 %copy-start.17 = (s32[128]{0:T(128)S(1)}, s32[128]{0:T(128)}, u32[]{:S(2)}) copy-start(s32[128]{0:T(128)} %param.12) | copy-start | bytes 1540
  14.2 10.6 %collective-permute-start.5 = (bf16[4,272,256]{2,1,0:T(8,128)(2,1)S(1)}, bf16[4,272,256]{2,1,0:T(8,128)(2,1)S(1)}, u32[]{:S(2)}, u32[]{:S(2)}) collective-permute-start(bf16[4,272,256]{2,1,0:T(8,128)(2,1)S(1)} %pad_maximum_fusion.1.rest_0_), channel_id=1, source_target_pairs={{0,24},{4,228},{8,0},{12,236},{16,8},{20,244},{24,16},{28,252},{32... | collective-permute-start | bytes 1671176 | tf_op jit(solution)/shard_map/ppermute | solution.py:64
  18.3 13.3 %collective-permute-start.4 = (bf16[4,272,256]{2,1,0:T(8,128)(2,1)S(1)}, bf16[4,272,256]{2,1,0:T(8,128)(2,1)S(1)}, u32[]{:S(2)}, u32[]{:S(2)}) collective-permute-start(bf16[4,272,256]{2,1,0:T(8,128)(2,1)S(1)} %pad_maximum_fusion.1.rest_0_), channel_id=1, source_target_pairs={{0,8},{4,36},{8,16},{12,44},{16,24},{20,52},{24,0},{28,60},{32,40}... | collective-permute-start | bytes 1671176 | tf_op jit(solution)/shard_map/ppermute | solution.py:64
  18.3 5.2 %collective-permute-start.6 = (bf16[2,272,256]{2,1,0:T(8,128)(2,1)S(1)}, bf16[2,272,256]{2,1,0:T(8,128)(2,1)S(1)}, u32[]{:S(2)}, u32[]{:S(2)}) collective-permute-start(bf16[2,272,256]{2,1,0:T(8,128)(2,1)S(1)} %pad_maximum_fusion.2), channel_id=1, source_target_pairs={{0,64},{8,72},{16,80},{24,88},{32,96},{40,104},{48,112},{56,120},{... | collective-permute-start | bytes 835592 | tf_op jit(solution)/shard_map/ppermute | solution.py:64
  19.0 4.5 %collective-permute-start.7 = (bf16[2,272,256]{2,1,0:T(8,128)(2,1)S(1)}, bf16[2,272,256]{2,1,0:T(8,128)(2,1)S(1)}, u32[]{:S(2)}, u32[]{:S(2)}) collective-permute-start(bf16[2,272,256]{2,1,0:T(8,128)(2,1)S(1)} %pad_maximum_fusion.3), channel_id=1, source_target_pairs={{0,192},{8,200},{16,208},{24,216},{32,224},{40,232},{48,240},{56,2... | collective-permute-start | bytes 835592 | tf_op jit(solution)/shard_map/ppermute | solution.py:64
  20.0 1.8 copy-start.16
  24.8 6.9 %copy-start.4 = (bf16[4,272,256]{2,1,0:T(8,128)(2,1)}, bf16[4,272,256]{2,1,0:T(8,128)(2,1)S(1)}, u32[]{:S(2)}) copy-start(bf16[4,272,256]{2,1,0:T(8,128)(2,1)S(1)} %collective-permute-done.5.rest_2_) | copy-start | bytes 1671172
  31.6 0.8 copy-start.8
  31.6 10.5 %copy-start.2 = (bf16[4,272,256]{2,1,0:T(8,128)(2,1)}, bf16[4,272,256]{2,1,0:T(8,128)(2,1)S(1)}, u32[]{:S(2)}) copy-start(bf16[4,272,256]{2,1,0:T(8,128)(2,1)S(1)} %constant_dynamic-update-slice_fusion.rest_2_) | copy-start | bytes 1671172
  31.7 10.4 %collective-permute-start.10 = (bf16[4,272,256]{2,1,0:T(8,128)(2,1)S(1)}, bf16[4,272,256]{2,1,0:T(8,128)(2,1)S(1)}, u32[]{:S(2)}, u32[]{:S(2)}) collective-permute-start(bf16[4,272,256]{2,1,0:T(8,128)(2,1)S(1)} %broadcast_select_fusion.2), channel_id=1, source_target_pairs={{0,24},{4,228},{8,0},{12,236},{16,8},{20,244},{24,16},{28,252},{32... | collective-permute-start | bytes 1671176 | tf_op jit(solution)/shard_map/ppermute | solution.py:64
  32.4 9.7 %collective-permute-start.9 = (bf16[4,272,256]{2,1,0:T(8,128)(2,1)S(1)}, bf16[4,272,256]{2,1,0:T(8,128)(2,1)S(1)}, u32[]{:S(2)}, u32[]{:S(2)}) collective-permute-start(bf16[4,272,256]{2,1,0:T(8,128)(2,1)S(1)} %collective-permute-done.4.rest_1_), channel_id=1, source_target_pairs={{0,8},{4,36},{8,16},{12,44},{16,24},{20,52},{24,0},{28,60},{32,40}... | collective-permute-start | bytes 1671176 | tf_op jit(solution)/shard_map/ppermute | solution.py:64
  42.1 2.8 %copy-start.9 = (bf16[4,272,256]{2,1,0:T(8,128)(2,1)}, bf16[4,272,256]{2,1,0:T(8,128)(2,1)S(1)}, u32[]{:S(2)}) copy-start(bf16[4,272,256]{2,1,0:T(8,128)(2,1)S(1)} %collective-permute-done.10.rest_1_) | copy-start | bytes 1671172
  42.1 2.8 %copy-start.5 = (bf16[4,272,256]{2,1,0:T(8,128)(2,1)}, bf16[4,272,256]{2,1,0:T(8,128)(2,1)S(1)}, u32[]{:S(2)}) copy-start(bf16[4,272,256]{2,1,0:T(8,128)(2,1)S(1)} %collective-permute-done.9.rest_0_) | copy-start | bytes 1671172
  42.1 10.0 %collective-permute-start.11 = (bf16[4,272,256]{2,1,0:T(8,128)(2,1)S(1)}, bf16[4,272,256]{2,1,0:T(8,128)(2,1)S(1)}, u32[]{:S(2)}, u32[]{:S(2)}) collective-permute-start(bf16[4,272,256]{2,1,0:T(8,128)(2,1)S(1)} %broadcast_select_fusion.1), channel_id=1, source_target_pairs={{0,8},{4,36},{8,16},{12,44},{16,24},{20,52},{24,0},{28,60},{32,40}... | collective-permute-start | bytes 1671176 | tf_op jit(solution)/shard_map/ppermute | solution.py:64
  42.2 9.9 %collective-permute-start.12 = (bf16[4,272,256]{2,1,0:T(8,128)(2,1)S(1)}, bf16[4,272,256]{2,1,0:T(8,128)(2,1)S(1)}, u32[]{:S(2)}, u32[]{:S(2)}) collective-permute-start(bf16[4,272,256]{2,1,0:T(8,128)(2,1)S(1)} %collective-permute-done.10.rest_1_), channel_id=1, source_target_pairs={{0,24},{4,228},{8,0},{12,236},{16,8},{20,244},{24,16},{28,252},{32... | collective-permute-start | bytes 1671176 | tf_op jit(solution)/shard_map/ppermute | solution.py:64
  52.1 6.8 %copy-start.6 = (bf16[4,272,256]{2,1,0:T(8,128)(2,1)}, bf16[4,272,256]{2,1,0:T(8,128)(2,1)S(1)}, u32[]{:S(2)}) copy-start(bf16[4,272,256]{2,1,0:T(8,128)(2,1)S(1)} %collective-permute-done.11.rest_0_) | copy-start | bytes 1671172
  52.1 6.8 %copy-start.7 = (bf16[4,272,256]{2,1,0:T(8,128)(2,1)}, bf16[4,272,256]{2,1,0:T(8,128)(2,1)S(1)}, u32[]{:S(2)}) copy-start(bf16[4,272,256]{2,1,0:T(8,128)(2,1)S(1)} %collective-permute-done.12.rest_1_) | copy-start | bytes 1671172
  52.2 11.1 %collective-permute-start.13 = (bf16[2,272,256]{2,1,0:T(8,128)(2,1)S(1)}, bf16[2,272,256]{2,1,0:T(8,128)(2,1)S(1)}, u32[]{:S(2)}, u32[]{:S(2)}) collective-permute-start(bf16[2,272,256]{2,1,0:T(8,128)(2,1)S(1)} %slice.60), channel_id=1, source_target_pairs={{4,36},{12,44},{20,52},{28,60},{36,68},{44,76},{52,84},{60,92},{68... | collective-permute-start | bytes 835592 | tf_op jit(solution)/shard_map/ppermute | solution.py:64
  54.3 9.1 %collective-permute-start.14 = (bf16[2,272,256]{2,1,0:T(8,128)(2,1)S(1)}, bf16[2,272,256]{2,1,0:T(8,128)(2,1)S(1)}, u32[]{:S(2)}, u32[]{:S(2)}) collective-permute-start(bf16[2,272,256]{2,1,0:T(8,128)(2,1)S(1)} %slice.61), channel_id=1, source_target_pairs={{4,228},{12,236},{20,244},{28,252},{36,4},{44,12},{52,20},{60,28},... | collective-permute-start | bytes 835592 | tf_op jit(solution)/shard_map/ppermute | solution.py:64
  63.3 0.7 copy-start.11
  63.3 0.8 copy-start.12
  68.3 6.5 %collective-permute-start.16 = (bf16[4,8,16,256]{3,2,1,0:T(8,128)(2,1)}, bf16[4,8,16,256]{3,2,1,0:T(8,128)(2,1)S(1)}, u32[]{:S(2)}, u32[]{:S(2)}) collective-permute-start(bf16[4,8,16,256]{3,2,1,0:T(8,128)(2,1)} %get-tuple-element.91), channel_id=1, source_target_pairs={{0,4},{4,0},{8,12},{12,8},{16,20},{20,16},{24,28},{28,24},{32,36},... | collective-permute-start | bytes 786440 | tf_op jit(solution)/shard_map/ppermute | solution.py:72
  73.4 2.5 %collective-permute-start.15 = (f32[2,128,256]{2,1,0:T(8,128)}, f32[2,128,256]{2,1,0:T(8,128)S(1)}, u32[]{:S(2)}, u32[]{:S(2)}) collective-permute-start(f32[2,128,256]{2,1,0:T(8,128)} %get-tuple-element.89), channel_id=1, source_target_pairs={{0,4},{4,0},{8,12},{12,8},{16,20},{20,16},{24,28},{28,24},{32,36},... | collective-permute-start | bytes 786440 | tf_op jit(solution)/shard_map/ppermute | solution.py:72
  75.8 0.9 copy-start.13
  75.8 1.0 copy-start.10
  76.8 10.3 %copy-start.14 = (bf16[256,256]{1,0:T(8,128)(2,1)S(1)}, bf16[256,256]{1,0:T(8,128)(2,1)}, u32[]{:S(2)}) copy-start(bf16[256,256]{1,0:T(8,128)(2,1)} %param.15) | copy-start | bytes 393220
  76.8 10.3 %copy-start.18 = (f32[256]{0:T(256)S(1)}, f32[256]{0:T(256)}, u32[]{:S(2)}) copy-start(f32[256]{0:T(256)} %param.10) | copy-start | bytes 3076
  77.7 6.3 %collective-permute-start.18 = (bf16[256,256]{1,0:T(8,128)(2,1)S(1)}, bf16[256,256]{1,0:T(8,128)(2,1)S(1)}, u32[]{:S(2)}, u32[]{:S(2)}) collective-permute-start(bf16[256,256]{1,0:T(8,128)(2,1)S(1)} %convolution_convert_fusion.1), channel_id=1, source_target_pairs={{0,2},{1,3},{2,0},{3,1},{4,6},{5,7},{6,4},{7,5},{8,10},{9,11},{10,... | collective-permute-start | bytes 393224 | tf_op jit(solution)/shard_map/ppermute | solution.py:76
  80.7 6.5 %collective-permute-start.19 = (bf16[256,256]{1,0:T(8,128)(2,1)S(1)}, bf16[256,256]{1,0:T(8,128)(2,1)S(1)}, u32[]{:S(2)}, u32[]{:S(2)}) collective-permute-start(bf16[256,256]{1,0:T(8,128)(2,1)S(1)} %convolution_convert_fusion), channel_id=1, source_target_pairs={{0,3},{1,0},{2,1},{3,2},{4,7},{5,4},{6,5},{7,6},{8,11},{9,8},{10,9... | collective-permute-start | bytes 393224 | tf_op jit(solution)/shard_map/ppermute | solution.py:76
  81.4 5.7 %collective-permute-start.17 = (bf16[256,256]{1,0:T(8,128)(2,1)S(1)}, bf16[256,256]{1,0:T(8,128)(2,1)S(1)}, u32[]{:S(2)}, u32[]{:S(2)}) collective-permute-start(bf16[256,256]{1,0:T(8,128)(2,1)S(1)} %convolution_convert_fusion.2), channel_id=1, source_target_pairs={{0,1},{1,2},{2,3},{3,0},{4,5},{5,6},{6,7},{7,4},{8,9},{9,10},{10,1... | collective-permute-start | bytes 393224 | tf_op jit(solution)/shard_map/ppermute | solution.py:76
  88.1 5.7 %collective-permute-start.22 = (bf16[256,256]{1,0:T(8,128)(2,1)S(1)}, bf16[256,256]{1,0:T(8,128)(2,1)S(1)}, u32[]{:S(2)}, u32[]{:S(2)}) collective-permute-start(bf16[256,256]{1,0:T(8,128)(2,1)S(1)} %get-tuple-element.122), channel_id=1, source_target_pairs={{0,1},{1,2},{2,3},{3,0},{4,5},{5,6},{6,7},{7,4},{8,9},{9,10},{10,1... | collective-permute-start | bytes 393224 | tf_op jit(solution)/shard_map/ppermute | solution.py:76
  89.9 8.5 %collective-permute-start.21 = (bf16[256,256]{1,0:T(8,128)(2,1)S(1)}, bf16[256,256]{1,0:T(8,128)(2,1)S(1)}, u32[]{:S(2)}, u32[]{:S(2)}) collective-permute-start(bf16[256,256]{1,0:T(8,128)(2,1)S(1)} %get-tuple-element.122), channel_id=1, source_target_pairs={{0,2},{1,3},{2,0},{3,1},{4,6},{5,7},{6,4},{7,5},{8,10},{9,11},{10,... | collective-permute-start | bytes 393224 | tf_op jit(solution)/shard_map/ppermute | solution.py:76
  92.5 6.1 %collective-permute-start.20 = (bf16[256,256]{1,0:T(8,128)(2,1)S(1)}, bf16[256,256]{1,0:T(8,128)(2,1)S(1)}, u32[]{:S(2)}, u32[]{:S(2)}) collective-permute-start(bf16[256,256]{1,0:T(8,128)(2,1)S(1)} %get-tuple-element.122), channel_id=1, source_target_pairs={{0,3},{1,0},{2,1},{3,2},{4,7},{5,4},{6,5},{7,6},{8,11},{9,8},{10,9... | collective-permute-start | bytes 393224 | tf_op jit(solution)/shard_map/ppermute | solution.py:76
  99.1 3.0 %collective-permute-start.23 = (f32[520,256]{1,0:T(8,128)S(1)}, f32[520,256]{1,0:T(8,128)S(1)}, u32[]{:S(2)}, u32[]{:S(2)}) collective-permute-start(f32[520,256]{1,0:T(8,128)S(1)} %select_maximum_fusion), channel_id=1, source_target_pairs={{0,4},{4,0},{8,12},{12,8},{16,20},{20,16},{24,28},{28,24},{32,36},... | collective-permute-start | bytes 1597448 | tf_op jit(solution)/shard_map/ppermute | solution.py:72
  100.7 2.2 %copy-start = (bf16[128,128,128]{2,1,0:T(8,128)(2,1)S(1)}, bf16[128,128,128]{2,1,0:T(8,128)(2,1)}, u32[]{:S(2)}) copy-start(bf16[128,128,128]{2,1,0:T(8,128)(2,1)} %own.11) | copy-start | bytes 12582916
  101.1 1.4 collective-permute-start.24
  102.1 0.9 copy-start.1
  105.0 15.2 %collective-permute-start.25 = (bf16[1104,256]{1,0:T(8,128)(2,1)S(1)}, bf16[1104,256]{1,0:T(8,128)(2,1)S(1)}, u32[]{:S(2)}, u32[]{:S(2)}) collective-permute-start(bf16[1104,256]{1,0:T(8,128)(2,1)S(1)} %get-tuple-element.95), channel_id=1, source_target_pairs={{4,36},{12,44},{20,52},{28,60},{36,68},{44,76},{52,84},{60,92},{68... | collective-permute-start | bytes 1695752 | tf_op jit(solution)/shard_map/ppermute | solution.py:64
  112.5 11.3 %collective-permute-start.27 = (bf16[1104,256]{1,0:T(8,128)(2,1)S(1)}, bf16[1104,256]{1,0:T(8,128)(2,1)S(1)}, u32[]{:S(2)}, u32[]{:S(2)}) collective-permute-start(bf16[1104,256]{1,0:T(8,128)(2,1)S(1)} %broadcast_select_fusion), channel_id=1, source_target_pairs={{0,24},{4,228},{8,0},{12,236},{16,8},{20,244},{24,16},{28,252},{32... | collective-permute-start | bytes 1695752 | tf_op jit(solution)/shard_map/ppermute | solution.py:64
  120.4 9.8 %collective-permute-start.26 = (bf16[1104,256]{1,0:T(8,128)(2,1)S(1)}, bf16[1104,256]{1,0:T(8,128)(2,1)S(1)}, u32[]{:S(2)}, u32[]{:S(2)}) collective-permute-start(bf16[1104,256]{1,0:T(8,128)(2,1)S(1)} %fusion.3), channel_id=1, source_target_pairs={{0,8},{4,36},{8,16},{12,44},{16,24},{20,52},{24,0},{28,60},{32,40}... | collective-permute-start | bytes 1695752 | tf_op jit(solution)/shard_map/ppermute | solution.py:64
  130.4 8.5 %collective-permute-start.29 = (bf16[1104,256]{1,0:T(8,128)(2,1)S(1)}, bf16[1104,256]{1,0:T(8,128)(2,1)S(1)}, u32[]{:S(2)}, u32[]{:S(2)}) collective-permute-start(bf16[1104,256]{1,0:T(8,128)(2,1)S(1)} %add_convert_fusion.2), channel_id=1, source_target_pairs={{0,24},{4,228},{8,0},{12,236},{16,8},{20,244},{24,16},{28,252},{32... | collective-permute-start | bytes 1695752 | tf_op jit(solution)/shard_map/ppermute | solution.py:64
  131.4 9.8 %collective-permute-start.28 = (bf16[1104,256]{1,0:T(8,128)(2,1)S(1)}, bf16[1104,256]{1,0:T(8,128)(2,1)S(1)}, u32[]{:S(2)}, u32[]{:S(2)}) collective-permute-start(bf16[1104,256]{1,0:T(8,128)(2,1)S(1)} %add_convert_fusion.3), channel_id=1, source_target_pairs={{0,8},{4,36},{8,16},{12,44},{16,24},{20,52},{24,0},{28,60},{32,40}... | collective-permute-start | bytes 1695752 | tf_op jit(solution)/shard_map/ppermute | solution.py:64
  141.4 12.8 %collective-permute-start.30 = (bf16[1104,256]{1,0:T(8,128)(2,1)S(1)}, bf16[1104,256]{1,0:T(8,128)(2,1)S(1)}, u32[]{:S(2)}, u32[]{:S(2)}) collective-permute-start(bf16[1104,256]{1,0:T(8,128)(2,1)S(1)} %add_convert_fusion.1), channel_id=1, source_target_pairs={{0,8},{4,36},{8,16},{12,44},{16,24},{20,52},{24,0},{28,60},{32,40}... | collective-permute-start | bytes 1695752 | tf_op jit(solution)/shard_map/ppermute | solution.py:64
  141.7 12.5 %collective-permute-start.31 = (bf16[1104,256]{1,0:T(8,128)(2,1)S(1)}, bf16[1104,256]{1,0:T(8,128)(2,1)S(1)}, u32[]{:S(2)}, u32[]{:S(2)}) collective-permute-start(bf16[1104,256]{1,0:T(8,128)(2,1)S(1)} %add_convert_fusion), channel_id=1, source_target_pairs={{0,24},{4,228},{8,0},{12,236},{16,8},{20,244},{24,16},{28,252},{32... | collective-permute-start | bytes 1695752 | tf_op jit(solution)/shard_map/ppermute | solution.py:64
  145.4 1.4 collective-permute-start.32
  146.1 0.7 collective-permute-start.33
  154.5 9.6 %collective-permute-start.34 = (bf16[288,256]{1,0:T(8,128)(2,1)S(1)}, bf16[288,256]{1,0:T(8,128)(2,1)S(1)}, u32[]{:S(2)}, u32[]{:S(2)}) collective-permute-start(bf16[288,256]{1,0:T(8,128)(2,1)S(1)} %get-tuple-element.115), channel_id=1, source_target_pairs={{0,32},{4,12},{8,40},{12,20},{16,48},{20,28},{24,56},{28,4},{32,64... | collective-permute-start | bytes 442376 | tf_op jit(solution)/shard_map/ppermute | solution.py:64
  156.4 7.6 %collective-permute-start.35 = (bf16[288,256]{1,0:T(8,128)(2,1)S(1)}, bf16[288,256]{1,0:T(8,128)(2,1)S(1)}, u32[]{:S(2)}, u32[]{:S(2)}) collective-permute-start(bf16[288,256]{1,0:T(8,128)(2,1)S(1)} %get-tuple-element.116), channel_id=1, source_target_pairs={{0,224},{4,28},{8,232},{12,4},{16,240},{20,12},{24,248},{28,20},{3... | collective-permute-start | bytes 442376 | tf_op jit(solution)/shard_map/ppermute | solution.py:64
  161.6 5.5 %collective-permute-start.36 = (bf16[288,256]{1,0:T(8,128)(2,1)S(1)}, bf16[288,256]{1,0:T(8,128)(2,1)S(1)}, u32[]{:S(2)}, u32[]{:S(2)}) collective-permute-start(bf16[288,256]{1,0:T(8,128)(2,1)S(1)} %get-tuple-element.117), channel_id=1, source_target_pairs={{0,64},{4,20},{8,72},{12,28},{16,80},{20,4},{24,88},{28,12},{32,96... | collective-permute-start | bytes 442376 | tf_op jit(solution)/shard_map/ppermute | solution.py:64
  167.8 11.4 %collective-permute-start.37 = (f32[1,256]{1,0:T(1,128)S(1)}, f32[1,256]{1,0:T(1,128)S(1)}, u32[]{:S(2)}, u32[]{:S(2)}) collective-permute-start(f32[1,256]{1,0:T(1,128)S(1)} %shard_map.124), channel_id=1, source_target_pairs={{0,4},{8,12},{16,20},{24,28},{32,36},{40,44},{48,52},{56,60},{64,6... | collective-permute-start | bytes 3080 | tf_op jit(solution)/shard_map/ppermute | solution.py:536
